TPU v7x, 32 devices: a whole 2x2x4 slice. The times are simulated.
32 devices in a mesh: dp: 2 (over x), space: 16 (over z, y, core).
Axes of the slice: x: 2, y: 2, z: 4, core: 2. Of those that a mesh axis runs over, the one named last changes fastest.
Arguments:
- inputs: float32 [2, 32, 128, 128, 128], P('dp', None, 'space'), may hold values from -6 to 6
- preact: float32 [2, 32, 128, 128, 128], P('dp', None, 'space'), may hold values from -6 to 6
- cotangent: float32 [2, 32, 128, 128, 128], P('dp', None, 'space'), may hold values from -6 to 6
- spectral_weight: float32 [32, 1024, 2048], P(None, 'space'), may hold values from -3 to 3
- skip_weight: float32 [32, 32], replicated, may hold values from -1 to 1
Outputs:
- input_grad: float32 [2, 32, 128, 128, 128], P('dp', None, 'space')
- weight_grad: float32 [32, 1024, 2048], P('dp', 'space')
- skip_grad: float32 [32, 32], replicated
All inputs are finite; a program needn't handle non-finite values.
Results may differ from a plain program's by a relative error of at most 0.00016.
Values sent between devices are 32-bit elements; how exact they have to be, the bound alone decides.
A program may use at most 256 MiB of HBM per device.

v0:
```python
import jax
import jax.numpy as jnp
from jax import lax
from jax.sharding import PartitionSpec as P

N = 128
MX = 32
MY = 64
MZ = 16


highest = lax.Precision.HIGHEST
tanh_scale = 0.7978845608028654
cubic_term = 0.044715


def gelu_slope(preact):
    bounded = jnp.tanh(tanh_scale * (preact + cubic_term * preact * preact * preact))
    return 0.5 * (1.0 + bounded) + 0.5 * preact * (1.0 - bounded * bounded) * tanh_scale * (
        1.0 + 3.0 * cubic_term * preact * preact
    )


def signed_modes(modes_count):
    positions = jnp.arange(modes_count, dtype=jnp.int32)
    return jnp.where(positions < modes_count // 2, positions, positions - modes_count)


def phases(frequency, grid_size):
    points = jnp.arange(grid_size, dtype=jnp.int32)
    product = jnp.mod(frequency[:, None] * points[None, :], grid_size)
    return 2.0 * jnp.pi / grid_size * product.astype(jnp.float32)


def make_tables(grid_size, modes_x, modes_y, modes_z):
    angle_y = phases(signed_modes(modes_y), grid_size)
    angle_z = phases(jnp.arange(modes_z, dtype=jnp.int32), grid_size)
    angle_x = phases(signed_modes(modes_x), grid_size)
    cos_y, sin_y = (jnp.cos(angle_y), jnp.sin(angle_y))
    cos_z, sin_z = (jnp.cos(angle_z), jnp.sin(angle_z))
    cos_x, sin_x = (jnp.cos(angle_x), jnp.sin(angle_x))
    forward_y = jnp.stack([cos_y.T, -sin_y.T], 1)
    forward_z = jnp.stack([jnp.stack([cos_z.T, -sin_z.T], 1), jnp.stack([sin_z.T, cos_z.T], 1)], 0)
    forward_x = jnp.stack([jnp.stack([cos_x.T, -sin_x.T], 1), jnp.stack([sin_x.T, cos_x.T], 1)], 0)
    inverse_x = jnp.stack([jnp.stack([cos_x, sin_x], 1), jnp.stack([-sin_x, cos_x], 1)], 0)
    inverse_z = jnp.stack([jnp.stack([cos_z, sin_z], 1), jnp.stack([-sin_z, cos_z], 1)], 0)
    inverse_y = jnp.stack([cos_y, -sin_y], 1)
    return (forward_y, forward_z, forward_x, inverse_x, inverse_z, inverse_y)


def transform_yz(field, forward_y, forward_z):
    halfway = jnp.einsum("bcxyz,yrj->bcxrjz", field, forward_y, precision=highest)
    mixed = jnp.einsum("bcxrjz,rzsn->sbcxnj", halfway, forward_z, precision=highest)
    return mixed.reshape(mixed.shape[:4] + (mixed.shape[4] * mixed.shape[5],))


def transform_x(stacked, forward_x, norm_scale):
    return jnp.einsum("rbcxk,rxsm->sbcmk", stacked, forward_x, precision=highest) * norm_scale


def weight_terms(spectra, input_spectra):
    real_part = jnp.einsum("bomk,bimk->mkoi", spectra[0], input_spectra[0], precision=highest)
    real_part = real_part + jnp.einsum(
        "bomk,bimk->mkoi", spectra[1], input_spectra[1], precision=highest
    )
    imag_part = jnp.einsum("bomk,bimk->mkoi", spectra[1], input_spectra[0], precision=highest)
    imag_part = imag_part - jnp.einsum(
        "bomk,bimk->mkoi", spectra[0], input_spectra[1], precision=highest
    )
    stacked = jnp.stack([real_part, imag_part], 2)
    return stacked.reshape(stacked.shape[0], stacked.shape[1], -1)


def mode_products(weights, spectra):
    channels = spectra.shape[2]
    pieces = weights.reshape(weights.shape[0], weights.shape[1], 2, channels, channels)
    weight_real = pieces[:, :, 0]
    weight_imag = pieces[:, :, 1]
    real_part = jnp.einsum("mkoi,bomk->bimk", weight_real, spectra[0], precision=highest)
    real_part = real_part + jnp.einsum(
        "mkoi,bomk->bimk", weight_imag, spectra[1], precision=highest
    )
    imag_part = jnp.einsum("mkoi,bomk->bimk", weight_real, spectra[1], precision=highest)
    imag_part = imag_part - jnp.einsum(
        "mkoi,bomk->bimk", weight_imag, spectra[0], precision=highest
    )
    return jnp.stack([real_part, imag_part], 0)


def restore_x(dual, inverse_x):
    return jnp.einsum("rbcmk,rmsx->sbcxk", dual, inverse_x, precision=highest)


def restore_yz(stacked, inverse_z, inverse_y):
    depth_modes = inverse_z.shape[1]
    shaped = stacked.reshape(stacked.shape[:4] + (depth_modes, stacked.shape[4] // depth_modes))
    planes = jnp.einsum("rbcxnj,rnsz->bcxjsz", shaped, inverse_z, precision=highest)
    return jnp.einsum("bcxjsz,jsy->bcxyz", planes, inverse_y, precision=highest)


def body(inputs, preact, cotangent, spectral_weight, skip_weight):
    norm_scale = float(N) ** (-1.5)
    tables = make_tables(N, MX, MY, MZ)
    grad_pre = cotangent * gelu_slope(preact)
    partial_grad = transform_yz(grad_pre, tables[0], tables[1])
    partial_input = transform_yz(inputs, tables[0], tables[1])
    spec_grad = transform_x(
        lax.all_to_all(partial_grad, "space", split_axis=4, concat_axis=3, tiled=True),
        tables[2],
        norm_scale,
    )
    spec_input = transform_x(
        lax.all_to_all(partial_input, "space", split_axis=4, concat_axis=3, tiled=True),
        tables[2],
        norm_scale,
    )
    weight_grad = lax.psum_scatter(
        weight_terms(spec_grad, spec_input), "dp", scatter_dimension=0, tiled=True
    )
    dual = mode_products(spectral_weight, spec_grad)
    along_x = restore_x(dual, tables[3])
    spatial = restore_yz(
        lax.all_to_all(along_x, "space", split_axis=3, concat_axis=4, tiled=True),
        tables[4],
        tables[5],
    )
    skip_term = jnp.einsum("oi,boxyz->bixyz", skip_weight, grad_pre, precision=highest)
    input_grad = norm_scale * spatial + skip_term
    local_skip = norm_scale * jnp.einsum("boxyz,bixyz->oi", grad_pre, inputs, precision=highest)
    skip_grad = lax.psum(local_skip, ("dp", "space"))
    return (input_grad, weight_grad, skip_grad)


def solution(mesh):
    in_specs = (
        P("dp", None, "space", None, None),
        P("dp", None, "space", None, None),
        P("dp", None, "space", None, None),
        P(None, "space", None),
        P(),
    )
    out_specs = (P("dp", None, "space", None, None), P("dp", "space", None), P())
    return jax.shard_map(body, mesh=mesh, in_specs=in_specs, out_specs=out_specs, check_vma=False)
```

profile of v0, /device:TPU:15, one launch (start us, length us, event | category | flops | bytes accessed | tf_op | source)
XLA Modules:
  0.0 670.4 jit_solution(1229228601111269783)
XLA Ops:
  7.3 0.2 fusion.104
  7.5 22.4 %fusion.28 = f32[32,8,2,64,128]{4,3,1,0,2:T(8,128)} fusion(f32[1,32,8,128,128]{4,3,2,1,0:T(8,128)} %param.5, f32[128,1,64]{0,2,1:T(8,128)S(1)} %get-tuple-element.48, f32[128,1,64]{0,2,1:T(8,128)S(1)} %get-tuple-element.47), kind=kOutput, calls=%fused_computation.37 | convolution fusion | flops 6442467328 | bytes 33619968 | tf_op jit(solution)/shard_map/bcxyz,yrj->bcxrjz/dot_general | solution.py:52
  30.0 26.5 %fusion.42 = f32[2,1,32,8,16,64]{5,4,3,2,0,1:T(8,128)} fusion(f32[32,8,2,64,128]{4,3,1,0,2:T(8,128)} %fusion.28, f32[1,128,2,16]{1,3,0,2:T(8,128)S(1)} %get-tuple-element.38, f32[1,128,2,16]{1,3,0,2:T(8,128)S(1)} %get-tuple-element.37), kind=kOutput, calls=%fused_computation.47 | convolution fusion | flops 1610620928 | bytes 18907136 | tf_op jit(solution)/shard_map/bcxrjz,rzsn->sbcxnj/dot_general | solution.py:53
  56.5 7.3 %copy.181 = f32[2,1,32,8,16,64]{2,3,0,5,4,1:T(8,128)} copy(f32[2,1,32,8,16,64]{5,4,3,2,0,1:T(8,128)} %fusion.42) | data formatting | bytes 4194304 | tf_op jit(solution)/shard_map/reshape | solution.py:54
  63.7 8.6 %reshape.753 = f32[16,1,32768]{2,1,0:T(1,128)} reshape(f32[1024,2,1,8,32]{4,3,2,1,0:T(8,128)} %bitcast.271) | data formatting | bytes 4194304
  72.3 7.2 %all-to-all-start.2 = ((f32[16,1,32768]{2,1,0:T(1,128)}), f32[16,1,32768]{2,1,0:T(1,128)S(1)}, u32[]{:S(2)}, u32[]{:S(2)}) async-start(f32[16,1,32768]{2,1,0:T(1,128)} %reshape.753), calls=%async_computation.2 | async-start | bytes 4194304 | tf_op jit(solution)/shard_map/all_to_all | solution.py:113
  79.5 31.9 %fusion.25 = f32[32,8,2,64,128]{4,3,1,0,2:T(8,128)} fusion(f32[128,1,64]{0,2,1:T(8,128)S(1)} %get-tuple-element.48, f32[128,1,64]{0,2,1:T(8,128)S(1)} %get-tuple-element.47, f32[1,32,8,128,128]{4,3,2,1,0:T(8,128)} %param.7, f32[1,32,8,128,128]{4,3,2,1,0:T(8,128)} %param.6), kind=kOutput, calls=%fused_computation.36 | convolution fusion | flops 6517964800 | bytes 50397184 | tf_op jit(solution)/shard_map/bcxyz,yrj->bcxrjz/dot_general | solution.py:52
  111.3 26.4 %fusion.39 = f32[2,1,32,8,16,64]{5,4,3,2,0,1:T(8,128)} fusion(f32[32,8,2,64,128]{4,3,1,0,2:T(8,128)} %fusion.25, f32[1,128,2,16]{1,3,0,2:T(8,128)S(1)} %get-tuple-element.38, f32[1,128,2,16]{1,3,0,2:T(8,128)S(1)} %get-tuple-element.37), kind=kOutput, calls=%fused_computation.46 | convolution fusion | flops 1610620928 | bytes 18907136 | tf_op jit(solution)/shard_map/bcxrjz,rzsn->sbcxnj/dot_general | solution.py:53
  137.7 7.3 %copy.173 = f32[2,1,32,8,16,64]{2,3,0,5,4,1:T(8,128)} copy(f32[2,1,32,8,16,64]{5,4,3,2,0,1:T(8,128)} %fusion.39) | data formatting | bytes 4194304 | tf_op jit(solution)/shard_map/reshape | solution.py:54
  145.0 8.6 %reshape.749 = f32[16,1,32768]{2,1,0:T(1,128)} reshape(f32[1024,2,1,8,32]{4,3,2,1,0:T(8,128)} %bitcast.272) | data formatting | bytes 4194304
  153.5 6.0 all-to-all-start
  159.6 23.1 %copy.106 = f32[32,64,2048]{1,2,0:T(8,128)} copy(f32[32,64,2048]{2,1,0:T(8,128)} %param.8) | data formatting | bytes 33554432 | tf_op args[3]
  182.7 0.2 fusion.129
  182.9 0.6 broadcast.846
  183.5 7.3 %reduce.9 = f32[16,32768]{1,0:T(8,128)S(1)} reduce(f32[16,1,32768]{2,1,0:T(1,128)} %copy-done.2, f32[]{:T(128)} %broadcast.846), dimensions={1}, to_apply=%all_to_all.39.reduce_sub_computation | reduce | bytes 4194308 | tf_op jit(solution)/shard_map/all_to_all | solution.py:113
  190.8 4.8 reshape.754
  195.6 7.5 %copy.182 = f32[2,1,32,8,16,64]{5,4,3,2,0,1:T(8,128)} copy(f32[2,1,32,8,16,64]{2,3,0,5,4,1:T(8,128)} %bitcast.273) | data formatting | bytes 4194304 | tf_op jit(solution)/shard_map/all_to_all | solution.py:113
  203.1 6.4 fusion.54
  209.6 1.1 copy.120
  210.7 1.1 copy.122
  211.8 7.3 %reduce.8 = f32[16,32768]{1,0:T(8,128)S(1)} reduce(f32[16,1,32768]{2,1,0:T(1,128)} %all-to-all-done, f32[]{:T(128)} %broadcast.846), dimensions={1}, to_apply=%all_to_all.33.reduce_sub_computation | reduce | bytes 4194308 | tf_op jit(solution)/shard_map/all_to_all | solution.py:108
  219.1 4.8 reshape.750
  223.9 7.5 %copy.174 = f32[2,1,32,8,16,64]{5,4,3,2,0,1:T(8,128)} copy(f32[2,1,32,8,16,64]{2,3,0,5,4,1:T(8,128)} %bitcast.274) | data formatting | bytes 4194304 | tf_op jit(solution)/shard_map/all_to_all | solution.py:108
  231.4 6.1 fusion.60
  237.6 1.1 copy.185
  238.7 1.1 copy.186
  239.8 22.0 %add_bitcast_fusion = (f32[32,64,1,32,32]{1,4,3,2,0:T(8,128)S(1)}, f32[32,64,1,32,32]{1,4,3,2,0:T(8,128)}, f32[32,64,32]{1,2,0:T(8,128)}, f32[32,64,32]{1,2,0:T(...) fusion(f32[32,64,32]{1,2,0:T(8,128)} %copy.186, f32[32,64,32]{1,2,0:T(8,128)} %copy.185, ...), kind=kLoop, calls=%fused_computation.32 | loop fusion | flops 29097984 | bytes 35651584 | tf_op jit(solution)/shard_map/stack | solution.py:70
  261.8 18.7 %pad_maximum_fusion = f32[32,64,2,32,32]{1,4,3,2,0:T(8,128)} fusion(f32[32,64,1,32,32]{1,4,3,2,0:T(8,128)} %get-tuple-element.22, f32[32,64,1,32,32]{1,4,3,2,0:T(8,128)S(1)} %get-tuple-element.21), kind=kLoop, calls=%fused_computation | loop fusion | flops 4194304 | bytes 33554432 | tf_op jit(solution)/shard_map/stack | solution.py:70
  280.8 0.8 copy-done.4
  281.6 0.2 copy-done.5
  281.8 0.6 fusion.76
  282.3 0.6 fusion.75
  282.9 1.8 convolution_bitcast_fusion
  284.8 4.5 copy.107
  289.2 5.5 reshape.751
  294.8 6.3 all-to-all-start.1
  301.1 15.1 %fusion.146 = f32[32,8,128,128]{3,2,1,0:T(8,128)S(1)} fusion(f32[1,32,8,128,128]{4,3,2,1,0:T(8,128)} %param.7, f32[1,32,8,128,128]{4,3,2,1,0:T(8,128)} %param.6), kind=kLoop, calls=%fused_computation.172 | loop fusion | flops 75497472 | bytes 50331648 | tf_op jit(solution)/shard_map/reshape
  316.2 6.2 copy-done.1
  322.4 37.5 %fusion.68 = f32[32,32]{1,0:T(8,128)S(1)} fusion(f32[32,8,128,128]{3,2,1,0:T(8,128)} %bitcast.270, f32[32,8,128,128]{3,2,1,0:T(8,128)S(1)} %fusion.146), kind=kOutput, calls=%fused_computation.56 | convolution fusion | flops 1610613760 | bytes 33558528 | tf_op jit(solution)/shard_map/boxyz,bixyz->oi/dot_general | solution.py:129
  359.9 40.0 %psum.7 = f32[32,32]{1,0:T(8,128)} all-reduce(f32[32,32]{1,0:T(8,128)S(1)} %fusion.68), channel_id=1, replica_groups=mesh['dp'=2,'space'=16] {'dp','space'}, use_global_device_ids=true, to_apply=%region_1.2 | all-reduce | flops 1024 | bytes 8192 | tf_op jit(solution)/shard_map/psum | solution.py:130
  400.1 0.2 fusion.109
  400.3 33.5 %fusion.21 = f32[8,128,128,32]{2,3,1,0:T(8,128)} fusion(f32[32,8,128,128]{3,2,1,0:T(8,128)} %copy-done.1, f32[32,32]{1,0:T(8,128)S(1)} %copy-done), kind=kOutput, calls=%fused_computation.34 | convolution fusion | flops 1610612736 | bytes 33558528 | tf_op jit(solution)/shard_map/oi,boxyz->bixyz/dot_general | solution.py:127
  433.8 7.3 %reduce.10 = f32[16,32768]{1,0:T(8,128)S(1)} reduce(f32[16,1,32768]{2,1,0:T(1,128)} %all-to-all-done.1, f32[]{:T(128)} %broadcast.846), dimensions={1}, to_apply=%all_to_all.36.reduce_sub_computation | reduce | bytes 4194308 | tf_op jit(solution)/shard_map/all_to_all | solution.py:123
  441.2 3.0 reshape.752
  444.2 17.3 %fusion.35 = f32[32,8,64,2,128,1]{4,2,5,3,1,0:T(8,128)} fusion(f32[2,32,8,16,64,1]{4,1,0,2,3,5:T(8,128)} %bitcast.275, f32[1,16,2,128]{3,1,0,2:T(8,128)S(1)} %get-tuple-element.36, f32[1,16,2,128]{3,1,0,2:T(8,128)S(1)} %get-tuple-element.35), kind=kOutput, calls=%fused_computation.42 | convolution fusion | flops 1610620928 | bytes 18907136 | tf_op jit(solution)/shard_map/rbcxnj,rnsz->bcxjsz/dot_general | solution.py:97
  461.5 32.5 %bitcast_add_fusion = f32[1,32,8,128,128]{4,3,2,1,0:T(8,128)} fusion(f32[8,128,128,32]{2,3,1,0:T(8,128)} %fusion.21, f32[32,8,64,2,128,1]{4,2,5,3,1,0:T(8,128)} %fusion.35, f32[64,1,128]{2,0,1:T(8,128)S(1)} %get-tuple-element.40, f32[64,1,128]{2,0,1:T(8,128)S(1)} %get-tuple-element.39), kind=kOutput, calls=%fused_computation.11 | convolution fusion | flops 6450855936 | bytes 50397184 | tf_op jit(solution)/shard_map/bcxjsz,jsy->bcxyz/dot_general | solution.py:98
  494.1 156.6 %reduce-scatter.2.cloned.1.call-done = f32[16,64,2048]{1,2,0:T(8,128)} async-done(((f32[32,64,2048]{1,2,0:T(8,128)}), f32[16,64,2048]{1,2,0:T(8,128)}) %reduce-scatter.2.cloned.1.call-update) | async-done | bytes 8388624 | tf_op jit(solution)/shard_map/reduce_scatter | solution.py:117
  650.7 12.7 %copy.126 = f32[16,64,2048]{2,1,0:T(8,128)} copy(f32[16,64,2048]{1,2,0:T(8,128)} %reduce-scatter.2.cloned.1.call-done) | data formatting | bytes 16777216
  (31 shorter events, 0.7 us)
Async XLA Ops:
  7.2 393.1 %copy-start = (f32[32,32]{1,0:T(8,128)S(1)}, f32[32,32]{1,0:T(8,128)}, u32[]{:S(2)}) copy-start(f32[32,32]{1,0:T(8,128)} %param.9) | copy-start | bytes 12292
  7.2 22.8 %copy-start.6 = (s32[64]{0:T(128)}, s32[64]{0:T(128)S(1)}, u32[]{:S(2)}) copy-start(s32[64]{0:T(128)S(1)} %compare_select_fusion.1) | copy-start | bytes 772
  72.3 81.2 %all-to-all-start.2 = ((f32[16,1,32768]{2,1,0:T(1,128)}), f32[16,1,32768]{2,1,0:T(1,128)S(1)}, u32[]{:S(2)}, u32[]{:S(2)}) async-start(f32[16,1,32768]{2,1,0:T(1,128)} %reshape.753), calls=%async_computation.2 | async-start | bytes 4194304 | tf_op jit(solution)/shard_map/all_to_all | solution.py:113
  153.5 29.2 %copy-start.2 = (f32[16,1,32768]{2,1,0:T(1,128)}, f32[16,1,32768]{2,1,0:T(1,128)S(1)}, u32[]{:S(2)}) copy-start(f32[16,1,32768]{2,1,0:T(1,128)S(1)} %all-to-all-done.2) | copy-start | bytes 6291460
  153.5 58.2 %all-to-all-start = ((f32[16,1,32768]{2,1,0:T(1,128)}), f32[16,1,32768]{2,1,0:T(1,128)}, u32[]{:S(2)}, u32[]{:S(2)}) async-start(f32[16,1,32768]{2,1,0:T(1,128)} %reshape.749), calls=%async_computation | async-start | bytes 4194304 | tf_op jit(solution)/shard_map/all_to_all | solution.py:108
  159.5 491.1 %reduce-scatter.2.cloned.1.call-start = ((), (), s32[]{:S(2)}) async-start(), calls=%async_computation.4 | async-start | bytes 50331648 | tf_op jit(solution)/shard_map/reduce_scatter | solution.py:117
  280.6 1.0 copy-start.4
  280.6 1.2 copy-start.5
  280.6 1.8 copy-start.3
  294.8 139.1 %all-to-all-start.1 = ((f32[16,1,32768]{2,1,0:T(1,128)}), f32[16,1,32768]{2,1,0:T(1,128)}, u32[]{:S(2)}, u32[]{:S(2)}) async-start(f32[16,1,32768]{2,1,0:T(1,128)} %reshape.751), calls=%async_computation.1 | async-start | bytes 4194304 | tf_op jit(solution)/shard_map/all_to_all | solution.py:123
  316.2 6.2 copy-start.1
  322.4 77.7 %copy-start.7 = (s32[64]{0:T(128)S(1)}, s32[64]{0:T(128)}, u32[]{:S(2)}) copy-start(s32[64]{0:T(128)} %copy-done.6) | copy-start | bytes 772
Sparse Core Ops, SparseCore 0:
  280.7 369.9 reduce-scatter.1
where the time goes:
time: 681 us; the launch traced here: 670 us
  matrix products  242 us (36%)
  waiting for transfers between devices  157 us (23%)
  local copies, waits for them, and re-layouts  117 us (17%)
  other arithmetic  80 us (12%)
  blocking collectives  40 us (6%)
  starting transfers between devices  19.6 us (3%)
  between operations  14.5 us (2%)
    reduce_scatter x1, waiting for transfers between devices, body(): lax.psum_scatter(weight_terms(spec_grad, spec_input), 'dp', scatter_dimen...  157 us
    unnamed x27, local copies, waits for them, and re-layouts  80.5 us
    dot_general x2, matrix products, transform_yz(): jnp.einsum('bcxyz,yrj->bcxrjz', field, forward_y, precision=highest)  54.3 us
    dot_general x2, matrix products, transform_yz(): jnp.einsum('bcxrjz,rzsn->sbcxnj', halfway, forward_z, precision=highest)  52.9 us
    another operation x2, other arithmetic, weight_terms(): stacked = jnp.stack([real_part, imag_part], 2)  40.7 us
    psum x1, blocking collectives, body(): skip_grad = lax.psum(local_skip, ('dp', 'space'))  40 us
    dot_general x1, matrix products, body(): jnp.einsum('boxyz,bixyz->oi', grad_pre, inputs, precision=highest)  37.5 us
    dot_general x1, matrix products, body(): jnp.einsum('oi,boxyz->bixyz', skip_weight, grad_pre, precision=highest)  33.5 us
  transfers between devices with their start and end apart: 4, of which 1 were waited for; matrix products, arithmetic and copies ran while one was open for 43% of the time, Pallas kernels for 0%

commit v1 on v0

v1 whole, which is shorter than its diff:
```python
import functools

import jax
import jax.numpy as jnp
import ml_dtypes
import numpy as np
from jax import lax
from jax.experimental import pallas as pl
from jax.experimental.pallas import tpu as pltpu
from jax.sharding import PartitionSpec as P

N = 128
C = 32
MX = 32
MY = 64
MZ = 16
NORM = float(N) ** -1.5

tanh_scale = 0.7978845608028654
cubic_term = 0.044715
BF = jnp.bfloat16
F32 = jnp.float32
LIMIT = 48 * 1024 * 1024


def signed(count):
    p = np.arange(count)
    return np.where(p < count // 2, p, p - count)


def waves(freq):
    angle = 2 * np.pi / N * np.mod(freq[:, None] * np.arange(N)[None, :], N)
    return np.cos(angle), np.sin(angle)


def halves(table):
    hi = table.astype(np.float32).astype(ml_dtypes.bfloat16)
    lo = (table - hi.astype(np.float64)).astype(np.float32).astype(ml_dtypes.bfloat16)
    return hi, lo


def make_tables():
    cx, sx = waves(signed(MX))
    cy, sy = waves(signed(MY))
    cz, sz = waves(np.arange(MZ))
    t = {}
    t["zf"] = np.concatenate(halves(np.concatenate([cz, -sz], 0)), 0)
    hi, lo = halves(np.block([[cy.T, -sy.T], [sy.T, cy.T]]))
    t["yf"] = np.concatenate([hi, hi, lo], 0)
    hi, lo = halves(np.concatenate([cx, sx], 0))
    t["xf"] = np.concatenate([hi, lo, hi], 1)
    t["xi"] = np.concatenate([hi.T, lo.T, hi.T], 1)
    hi, lo = halves(np.block([[cy, sy], [-sy, cy]]))
    t["yi"] = np.concatenate([hi, hi, lo], 0)
    hi, lo = halves(np.concatenate([cz, -sz], 0))
    t["zi"] = np.concatenate([hi, hi, lo], 0)
    eye = np.eye(C)
    spread_out = np.repeat(eye, C, axis=1)
    spread_in = np.tile(eye, (1, C))
    t["eo"] = np.concatenate([spread_out, spread_out], 0).astype(ml_dtypes.bfloat16)
    t["ei"] = np.concatenate([spread_in, spread_in], 0).astype(ml_dtypes.bfloat16)
    return t


def split(x):
    hi = x.astype(BF)
    lo = (x - hi.astype(F32)).astype(BF)
    return hi, lo


def nn(a, b):
    return lax.dot_general(a, b, (((1,), (0,)), ((), ())), preferred_element_type=F32)


def nt(a, b):
    return lax.dot_general(a, b, (((1,), (1,)), ((), ())), preferred_element_type=F32)


def tn(a, b):
    return lax.dot_general(a, b, (((0,), (0,)), ((), ())), preferred_element_type=F32)


def gelu_slope(h):
    t = jnp.tanh(tanh_scale * (h + cubic_term * h * h * h))
    return 0.5 * (1.0 + t) + 0.5 * h * (1.0 - t * t) * tanh_scale * (1.0 + 3.0 * cubic_term * h * h)


GROUP = 8


def planes_forward(d, first, zf_ref, yf_ref, out2d):
    hi, lo = split(d.reshape(GROUP * N, N))
    a = nt(zf_ref[...], hi)
    z = a[: 2 * MZ] + a[2 * MZ :] + nt(zf_ref[: 2 * MZ, :], lo)
    rows = []
    for c in range(GROUP):
        cols = slice(c * N, (c + 1) * N)
        rows.append(jnp.concatenate([z[:MZ, cols], z[MZ:, cols]], 1))
    hi, lo = split(jnp.concatenate(rows, 0))
    y = nn(jnp.concatenate([hi, lo, hi], 1), yf_ref[...])
    for c in range(GROUP):
        out2d[pl.ds(first + c, MZ, stride=C), :] = y[c * MZ : (c + 1) * MZ, :]


def grad_kernel(pre_ref, cot_ref, zf_ref, yf_ref, gp_ref, out_ref):
    out2d = out_ref.reshape(MZ * C, 2 * MY)
    for g in range(0, C, GROUP):
        gp = cot_ref[0, g : g + GROUP, 0] * gelu_slope(pre_ref[0, g : g + GROUP, 0])
        gp_ref[0, g : g + GROUP, 0] = gp
        planes_forward(gp, g, zf_ref, yf_ref, out2d)


def input_kernel(in_ref, gp_ref, zf_ref, yf_ref, out_ref, acc_ref):
    out2d = out_ref.reshape(MZ * C, 2 * MY)

    @pl.when(pl.program_id(0) == 0)
    def _():
        acc_ref[...] = jnp.zeros_like(acc_ref)

    for g in range(0, C, GROUP):
        planes_forward(in_ref[0, g : g + GROUP, 0], g, zf_ref, yf_ref, out2d)

    def rows(ref, y):
        a = ref[0, :, 0, pl.ds(y, 8), :].reshape(C * 8, N)
        b = ref[0, :, 0, pl.ds(y + 8, 8), :].reshape(C * 8, N)
        return split(jnp.concatenate([a, b], 1))

    @pl.loop(0, N // 16)
    def _(s):
        y = pl.multiple_of(s * 16, 16)
        gh, gl = rows(gp_ref, y)
        ih, il = rows(in_ref, y)
        acc_ref[...] += nt(
            jnp.concatenate([gh, gl, gh], 1), jnp.concatenate([ih, ih, il], 1)
        )


def swap(x):
    return pltpu.roll(x, MY, 1)


def lane_sign(rows, first):
    lane = lax.broadcasted_iota(jnp.int32, (rows, 2 * MY), 1)
    return jnp.where(lane < MY, first, -first).astype(F32)


def x_forward(a2d, xf_ref):
    for c in range(C):
        hi, lo = split(a2d[pl.ds(c, N, stride=C), :])
        p = nn(xf_ref[...], jnp.concatenate([hi, hi, lo], 0))
        s = (p[:MX] + lane_sign(MX, 1.0) * swap(p[MX:])) * NORM
        yield c, s


def modes_kernel(a_ref, w_ref, xf_ref, xi_ref, eo_ref, s_ref, out_ref, d_ref, *, dp, step):
    mh = MX // dp
    a2d = a_ref.reshape(N * C, 2 * MY)
    s2d = s_ref.reshape(MX * C, 2 * MY)
    out2d = out_ref.reshape(N * C, 2 * MY)
    pid = pl.program_id(0)

    @pl.when(pid == 0)
    def _():
        for c, s in x_forward(a2d, xf_ref):
            for h in range(dp):
                s_ref[h, c] = s[h * mh : (h + 1) * mh]

    for u in range(step):
        m = pid * step + u
        start = (m // mh) * (C * mh) + m % mh
        hi, lo = split(s2d[pl.ds(start, C, stride=mh), :])
        g = tn(jnp.concatenate([hi, lo], 0), eo_ref[...])
        gr, gi = g[:MY], g[MY:]
        wr, wi = w_ref[u, :, : C * C], w_ref[u, :, C * C :]

        def fold(x):
            total = x[:, :128]
            for t in range(1, C * C // 128):
                total = total + x[:, t * 128 : (t + 1) * 128]
            return total

        both = jnp.concatenate([fold(wr * gr + wi * gi), fold(wr * gi - wi * gr)], 0).T
        total = both[:C] + both[C : 2 * C] + both[2 * C : 3 * C] + both[3 * C :]
        d_ref[pl.ds(m, C, stride=MX), :] = total * NORM

    @pl.when(pid == MX // step - 1)
    def _():
        for i in range(C):
            d = d_ref[i * MX : (i + 1) * MX, :]
            hi, lo = split(jnp.concatenate([d, lane_sign(MX, -1.0) * swap(d)], 0))
            out2d[pl.ds(i, N, stride=C), :] = nn(xi_ref[...], jnp.concatenate([hi, hi, lo], 0))


def spectrum_kernel(a_ref, xf_ref, s_ref, *, dp):
    mh = MX // dp
    a2d = a_ref.reshape(N * C, 2 * MY)
    for c, s in x_forward(a2d, xf_ref):
        for h in range(dp):
            s_ref[h, c] = s[h * mh : (h + 1) * mh]


def weight_kernel(g_ref, i_ref, eo_ref, ei_ref, out_ref, *, dp, step):
    mh = MX // dp
    g2d = g_ref.reshape(MX * C, 2 * MY)
    i2d = i_ref.reshape(MX * C, 2 * MY)
    for u in range(step):
        m = pl.program_id(0) * step + u
        real = imag = None
        for b in range(dp):
            at = pl.ds(b * (C * mh) + m, C, stride=mh)
            g = tn(jnp.concatenate(split(g2d[at, :]), 0), eo_ref[...])
            i = tn(jnp.concatenate(split(i2d[at, :]), 0), ei_ref[...])
            gr, gi, ir, ii = g[:MY], g[MY:], i[:MY], i[MY:]
            r = gr * ir + gi * ii
            j = gi * ir - gr * ii
            real, imag = (r, j) if real is None else (real + r, imag + j)
        out_ref[u, :, : C * C] = real
        out_ref[u, :, C * C :] = imag


def inverse_kernel(b_ref, gp_ref, k_ref, yi_ref, zi_ref, out_ref, re_ref, im_ref):
    hi, lo = split(b_ref.reshape(MZ * C, 2 * MY)[...])
    v = nn(jnp.concatenate([hi, lo, hi], 1), yi_ref[...])
    re_ref[...] = v[:, :N]
    im_ref[...] = v[:, N:]
    for i in range(C):
        at = pl.ds(i, MZ, stride=C)
        hi, lo = split(jnp.concatenate([re_ref[at, :], im_ref[at, :]], 0))
        out_ref[0, i, 0] = tn(jnp.concatenate([hi, lo, hi], 0), zi_ref[...])
    kh, kl = split(k_ref[...])
    k3 = jnp.concatenate([kh, kl, kh], 1)

    @pl.loop(0, N // 16)
    def _(s):
        y = pl.multiple_of(s * 16, 16)
        a = gp_ref[0, :, 0, pl.ds(y, 8), :].reshape(C * 8, N)
        b = gp_ref[0, :, 0, pl.ds(y + 8, 8), :].reshape(C * 8, N)
        gh, gl = split(jnp.concatenate([a, b], 1))
        r = nn(k3, jnp.concatenate([gh, gh, gl], 0))
        out_ref[0, :, 0, pl.ds(y, 8), :] += r[:, :N].reshape(C, 8, N)
        out_ref[0, :, 0, pl.ds(y + 8, 8), :] += r[:, N:].reshape(C, 8, N)


def whole(shape):
    return pl.BlockSpec(shape, lambda *_: (0,) * len(shape))


def params():
    return pltpu.CompilerParams(vmem_limit_bytes=LIMIT)


def cost(flops, nbytes):
    return pl.CostEstimate(flops=int(flops), bytes_accessed=int(nbytes), transcendentals=0)


def body(space, dp, inputs, preact, cotangent, spectral_weight, skip_weight):
    t = {k: jnp.asarray(v) for k, v in make_tables().items()}
    xl = inputs.shape[2]
    kl = spectral_weight.shape[1]
    field = jax.ShapeDtypeStruct(inputs.shape, F32)
    spread = jax.ShapeDtypeStruct((MZ, xl, C, 2 * MY), F32)
    plane = pl.BlockSpec((1, C, 1, N, N), lambda x: (0, 0, x, 0, 0))
    lines = pl.BlockSpec((MZ, 1, C, 2 * MY), lambda x: (0, x, 0, 0))
    nbytes = inputs.size * 4

    gp, part_g = pl.pallas_call(
        grad_kernel,
        grid=(xl,),
        in_specs=[plane, plane, whole(t["zf"].shape), whole(t["yf"].shape)],
        out_specs=[plane, lines],
        out_shape=[field, spread],
        compiler_params=params(),
        cost_estimate=cost(nbytes * 300, nbytes * 4),
        name="grad_forward",
    )(preact, cotangent, t["zf"], t["yf"])
    part_i, acc = pl.pallas_call(
        input_kernel,
        grid=(xl,),
        in_specs=[plane, plane, whole(t["zf"].shape), whole(t["yf"].shape)],
        out_specs=[lines, whole((C * 8, C * 8))],
        out_shape=[spread, jax.ShapeDtypeStruct((C * 8, C * 8), F32)],
        compiler_params=params(),
        cost_estimate=cost(nbytes * 600, nbytes * 3),
        name="input_forward",
    )(inputs, gp, t["zf"], t["yf"])
    diag = jnp.einsum("oyiy->oi", acc.reshape(C, 8, C, 8), precision=lax.Precision.HIGHEST)
    skip_grad = lax.psum(NORM * diag, ("dp", "space"))

    q = space // MZ
    jl = MY // q

    def outward(part):
        p = part.reshape(MZ, xl, C, 2, q, jl).transpose(0, 4, 1, 2, 3, 5)
        p = p.reshape(space, xl, C, 2 * jl)
        return lax.all_to_all(p, "space", split_axis=0, concat_axis=0, tiled=True)

    arrived_g = outward(part_g)
    arrived_i = outward(part_i)
    mh = MX // dp

    if jl == MY and xl == 8:
        step = 4
        spec_shape = (dp, C, mh, 2 * MY)
        spec_g, along = pl.pallas_call(
            functools.partial(modes_kernel, dp=dp, step=step),
            grid=(MX // step,),
            in_specs=[
                whole(arrived_g.shape),
                pl.BlockSpec((step, kl, 2 * C * C), lambda m: (m, 0, 0)),
                whole(t["xf"].shape),
                whole(t["xi"].shape),
                whole(t["eo"].shape),
            ],
            out_specs=[whole(spec_shape), whole(arrived_g.shape)],
            out_shape=[
                jax.ShapeDtypeStruct(spec_shape, F32),
                jax.ShapeDtypeStruct(arrived_g.shape, F32),
            ],
            scratch_shapes=[pltpu.VMEM((C * MX, 2 * MY), F32)],
            compiler_params=params(),
            cost_estimate=cost(1e9, spectral_weight.size * 4 + arrived_g.size * 8),
            name="modes",
        )(arrived_g, spectral_weight, t["xf"], t["xi"], t["eo"])
        spec_i = pl.pallas_call(
            functools.partial(spectrum_kernel, dp=dp),
            in_specs=[whole(arrived_i.shape), whole(t["xf"].shape)],
            out_specs=whole(spec_shape),
            out_shape=jax.ShapeDtypeStruct(spec_shape, F32),
            grid=(1,),
            compiler_params=params(),
            cost_estimate=cost(1e8, arrived_i.size * 5),
            name="spectrum",
        )(arrived_i, t["xf"])
        both_g = lax.all_to_all(spec_g, "dp", split_axis=0, concat_axis=0, tiled=True)
        both_i = lax.all_to_all(spec_i, "dp", split_axis=0, concat_axis=0, tiled=True)
        wstep = 2
        weight_grad = pl.pallas_call(
            functools.partial(weight_kernel, dp=dp, step=wstep),
            grid=(mh // wstep,),
            in_specs=[whole(spec_shape), whole(spec_shape)]
            + [whole(t["eo"].shape), whole(t["ei"].shape)],
            out_specs=pl.BlockSpec((wstep, kl, 2 * C * C), lambda m: (m, 0, 0)),
            out_shape=jax.ShapeDtypeStruct((mh, kl, 2 * C * C), F32),
            compiler_params=params(),
            cost_estimate=cost(1e9, mh * kl * 2 * C * C * 4),
            name="weight_grad",
        )(both_g, both_i, t["eo"], t["ei"])
    else:
        weight_grad, along = modes_plain(space, dp, arrived_g, arrived_i, spectral_weight, jl)

    back = lax.all_to_all(along, "space", split_axis=0, concat_axis=0, tiled=True)
    back = back.reshape(MZ, q, xl, C, 2, jl).transpose(0, 2, 3, 4, 1, 5).reshape(MZ, xl, C, 2 * MY)
    kron = jnp.kron(skip_weight.T, jnp.eye(8, dtype=F32))
    input_grad = pl.pallas_call(
        inverse_kernel,
        grid=(xl,),
        in_specs=[lines, plane, whole(kron.shape), whole(t["yi"].shape), whole(t["zi"].shape)],
        out_specs=plane,
        out_shape=field,
        scratch_shapes=[pltpu.VMEM((MZ * C, N), F32)] * 2,
        compiler_params=params(),
        cost_estimate=cost(nbytes * 600, nbytes * 2),
        name="inverse",
    )(back, gp, kron, t["yi"], t["zi"])
    return input_grad, weight_grad, skip_grad


def modes_plain(space, dp, arrived_g, arrived_i, weights, jl):
    cx, sx = waves(signed(MX))
    fwd = jnp.asarray(np.stack([np.stack([cx.T, -sx.T], 1), np.stack([sx.T, cx.T], 1)], 0), F32)
    inv = jnp.asarray(np.stack([np.stack([cx, sx], 1), np.stack([-sx, cx], 1)], 0), F32)
    ein = functools.partial(jnp.einsum, precision=lax.Precision.HIGHEST)

    def spectrum(a):
        return ein("xcrj,rxsm->scmj", a.reshape(N, C, 2, jl), fwd) * NORM

    g, i = spectrum(arrived_g), spectrum(arrived_i)

    def other(s):
        return lax.all_to_all(s[None], "dp", split_axis=3, concat_axis=0, tiled=True)

    bg, bi = other(g), other(i)
    real = ein("bomk,bimk->mkoi", bg[:, 0], bi[:, 0]) + ein("bomk,bimk->mkoi", bg[:, 1], bi[:, 1])
    imag = ein("bomk,bimk->mkoi", bg[:, 1], bi[:, 0]) - ein("bomk,bimk->mkoi", bg[:, 0], bi[:, 1])
    weight_grad = jnp.stack([real, imag], 2).reshape(MX // dp, jl, 2 * C * C)
    w = weights.reshape(MX, jl, 2, C, C)
    dr = ein("mkoi,omk->imk", w[:, :, 0], g[0]) + ein("mkoi,omk->imk", w[:, :, 1], g[1])
    di = ein("mkoi,omk->imk", w[:, :, 0], g[1]) - ein("mkoi,omk->imk", w[:, :, 1], g[0])
    along = ein("rimk,rmsx->xisk", jnp.stack([dr, di], 0), inv) * NORM
    return weight_grad, along.reshape(arrived_g.shape)


def solution(mesh):
    in_specs = (
        P("dp", None, "space", None, None),
        P("dp", None, "space", None, None),
        P("dp", None, "space", None, None),
        P(None, "space", None),
        P(),
    )
    out_specs = (P("dp", None, "space", None, None), P("dp", "space", None), P())
    local = functools.partial(body, mesh.shape["space"], mesh.shape["dp"])
    return jax.shard_map(local, mesh=mesh, in_specs=in_specs, out_specs=out_specs, check_vma=False)
```

time: 681 us -> 274 us (0.40)
  matrix products: 242 us -> 0 us
  Pallas kernels: 0 us -> 115 us
  waiting for transfers between devices: 157 us -> 44.3 us
  local copies, waits for them, and re-layouts: 117 us -> 21 us
  other arithmetic: 80 us -> 5.32 us
  blocking collectives: 40 us -> 61.9 us
  between operations: 14.5 us -> 0.72 us
    dot_general x11 -> x0, matrix products: 242 us -> none  [the longest x2 54.3 us: transform_yz(): jnp.einsum('bcxyz,yrj->bcxrjz', field, forward_y, precision=highest)]
    reduce_scatter x1 -> x0, waiting for transfers between devices: 157 us -> none  [body(): lax.psum_scatter(weight_terms(spec_grad, spec_input), 'dp', scatter_dimen...]
    pallas_call x0 -> x6, Pallas kernels: none -> 115 us  [the longest x1 34.1 us: body(): pl.pallas_call(input_kernel, grid=(xl,), in_specs=[plane, plane, whole(t[...]
    unnamed x27 -> x34, local copies, waits for them, and re-layouts: 80.5 us -> 11.9 us
    all_to_all x3 -> x4, waiting for transfers between devices: 0.01 us -> 44.3 us  [the longest x2 40.7 us: outward(): return lax.all_to_all(p, 'space', split_axis=0, concat_axis=0, tiled=True)]
    another operation x8 -> x0, other arithmetic: 41.9 us -> none  [the longest x2 40.7 us: weight_terms(): stacked = jnp.stack([real_part, imag_part], 2)]
    all_to_all x3 -> x0, other arithmetic: 22 us -> none  [the longest x1 7.33 us: body(): lax.all_to_all(along_x, 'space', split_axis=3, concat_axis=4, tiled=True)]
    all_to_all x3 -> x0, local copies, waits for them, and re-layouts: 15.5 us -> none  [the longest x2 8.05 us: body(): lax.all_to_all(partial_grad, 'space', split_axis=4, concat_axis=3, tiled=...]
  transfers between devices with their start and end apart: 4 -> 4, of which waited for: 1 -> 3; matrix products, arithmetic and copies ran while one was open for 43% -> 5% of each run, Pallas kernels for 0% -> 22%
where the time goes in v1:
time: 274 us; the launch traced here: 269 us
  Pallas kernels  115 us (42%)
  blocking collectives  61.9 us (23%)
  waiting for transfers between devices  44.3 us (16%)
  starting transfers between devices  21.7 us (8%)
  local copies, waits for them, and re-layouts  21 us (8%)
  other arithmetic  5.32 us (2%)
    psum x1, blocking collectives, body(): skip_grad = lax.psum(NORM * diag, ('dp', 'space'))  52.6 us
    all_to_all x2, waiting for transfers between devices, outward(): return lax.all_to_all(p, 'space', split_axis=0, concat_axis=0, tiled=True)  40.7 us
    pallas_call x1, Pallas kernels, body(): pl.pallas_call(input_kernel, grid=(xl,), in_specs=[plane, plane, whole(t[...  34.1 us
    pallas_call x1, Pallas kernels, body(): pl.pallas_call(inverse_kernel, grid=(xl,), in_specs=[lines, plane, whole(...  29.5 us
    pallas_call x1, Pallas kernels, body(): pl.pallas_call(grad_kernel, grid=(xl,), in_specs=[plane, plane, whole(t['...  24.6 us
    pallas_call x1, Pallas kernels, body(): pl.pallas_call(functools.partial(modes_kernel, dp=dp, step=step), grid=(M...  15.7 us
    unnamed x34, local copies, waits for them, and re-layouts  11.9 us
    all_to_all x2, starting transfers between devices, outward(): return lax.all_to_all(p, 'space', split_axis=0, concat_axis=0, tiled=True)  11.6 us
  transfers between devices with their start and end apart: 4, of which 3 were waited for; matrix products, arithmetic and copies ran while one was open for 5% of the time, Pallas kernels for 22%

profile of v1, /device:TPU:15, one launch (start us, length us, event | category | flops | bytes accessed | tf_op | source)
XLA Modules:
  0.0 269.4 jit_solution(5666777284926437138)
XLA Ops:
  0.6 0.0 copy-start.7
  0.6 0.9 copy-done.7
  1.6 0.0 copy-start.13
  1.6 0.7 copy-done.13
  2.3 24.6 %grad_forward.1 = (f32[1,32,8,128,128]{4,3,2,1,0:T(8,128)}, f32[16,8,32,128]{3,2,1,0:T(8,128)S(1)}) custom-call(f32[1,32,8,128,128]{4,3,2,1,0:T(8,128)} %pre_ref.1, f32[1,32,8,128,128]{4,3,2,1,0:T(8,128)} %cot_ref.1, bf16[64,128]{1,0:T(8,128)(2,1)S(1)} %copy-done.13, bf16[768,128]{1,0:T(8,128)(2,1)S(1)} %copy-done.7), custom_call_target="tpu_custom_call" | custom-call | flops 5033164800 | bytes 67108864 | tf_op jit(solution)/shard_map/grad_forward/pallas_call | solution.py:266
  26.9 0.0 copy-start.4
  26.9 1.3 copy-done.4
  28.2 0.0 copy-start.8
  28.2 0.0 copy-start.14
  28.2 6.7 %all-to-all-start = ((f32[16,8,32,128]{3,2,1,0:T(8,128)}), f32[16,8,32,128]{3,2,1,0:T(8,128)S(1)}, u32[]{:S(2)}, u32[]{:S(2)}) async-start(f32[16,8,32,128]{3,2,1,0:T(8,128)} %copy-done.4), calls=%async_computation | async-start | bytes 4194304 | tf_op jit(solution)/shard_map/all_to_all | solution.py:295
  34.9 0.0 copy-done.8
  34.9 0.0 copy-done.14
  34.9 34.1 %input_forward.1 = (f32[16,8,32,128]{3,2,1,0:T(8,128)S(1)}, f32[256,256]{1,0:T(8,128)S(1)}) custom-call(f32[1,32,8,128,128]{4,3,2,1,0:T(8,128)} %in_ref.1, f32[1,32,8,128,128]{4,3,2,1,0:T(8,128)} %get-tuple-element.11.gp_ref, bf16[64,128]{1,0:T(8,128)(2,1)S(1)} %copy-done.14, bf16[768,128]{1,0:T(8,128)(2,1)S(1)} %copy-done.8), custom_call_target="tpu_custom_call" | custom-call | flops 10066329600 | bytes 50331648 | tf_op jit(solution)/shard_map/input_forward/pallas_call | solution.py:276
  69.0 0.0 copy-start.3
  69.0 1.3 copy-done.3
  70.3 0.0 copy-start.5
  70.3 0.0 copy-start.9
  70.3 0.0 copy-start.12
  70.3 12.0 %all-to-all-done.a_ref = f32[16,8,32,128]{3,2,1,0:T(8,128)S(1)} async-done(((f32[16,8,32,128]{3,2,1,0:T(8,128)}), f32[16,8,32,128]{3,2,1,0:T(8,128)S(1)}, u32[]{:S(2)}, u32[]{:S(2)}) %all-to-all-start) | async-done | bytes 2097184 | tf_op jit(solution)/shard_map/all_to_all | solution.py:295
  82.3 1.3 copy-done
  83.6 4.9 %all-to-all-start.3 = ((f32[16,8,32,128]{3,2,1,0:T(8,128)}), f32[16,8,32,128]{3,2,1,0:T(8,128)S(1)}, u32[]{:S(2)}, u32[]{:S(2)}) async-start(f32[16,8,32,128]{3,2,1,0:T(8,128)} %copy-done.3), calls=%async_computation.3 | async-start | bytes 4194304 | tf_op jit(solution)/shard_map/all_to_all | solution.py:295
  88.5 0.0 copy-done.5
  88.5 0.0 copy-done.9
  88.5 0.0 copy-done.12
  88.6 0.0 copy-start.1
  88.6 1.6 copy-done.1
  90.2 15.7 %modes.1 = (f32[2,32,16,128]{3,2,1,0:T(8,128)}, f32[16,8,32,128]{3,2,1,0:T(8,128)S(1)}) custom-call(f32[16,8,32,128]{3,2,1,0:T(8,128)S(1)} %copy-done.1, f32[32,64,2048]{2,1,0:T(8,128)} %w_ref.1, bf16[64,384]{1,0:T(8,128)(2,1)S(1)} %copy-done.9, bf16[128,192]{1,0:T(8,128)(2,1)S(1)} %copy-done.12, bf16[64,1024]{1,0:T(8,128)(2,1)S(1)} %copy-done.5), custom_call_target="tpu_custom_call" | custom-call | flops 1000000000 | bytes 20971520 | tf_op jit(solution)/shard_map/modes/pallas_call | solution.py:304
  105.9 1.3 copy-done.2
  107.2 28.7 %all-to-all-done.3.a_ref = f32[16,8,32,128]{3,2,1,0:T(8,128)S(1)} async-done(((f32[16,8,32,128]{3,2,1,0:T(8,128)}), f32[16,8,32,128]{3,2,1,0:T(8,128)S(1)}, u32[]{:S(2)}, u32[]{:S(2)}) %all-to-all-start.3) | async-done | bytes 2097184 | tf_op jit(solution)/shard_map/all_to_all | solution.py:295
  135.9 3.7 %all-to-all-start.2 = ((f32[2,32,16,128]{3,2,1,0:T(8,128)}), f32[2,32,16,128]{3,2,1,0:T(8,128)S(1)}, u32[]{:S(2)}, u32[]{:S(2)}) async-start(f32[2,32,16,128]{3,2,1,0:T(8,128)} %get-tuple-element.12), calls=%async_computation.2 | async-start | bytes 1048576 | tf_op jit(solution)/shard_map/all_to_all | solution.py:334
  139.7 0.8 copy-done.10
  140.5 2.4 spectrum.1
  142.9 3.5 %all-to-all-done.2.g_ref = f32[2,32,16,128]{3,2,1,0:T(8,128)S(1)} async-done(((f32[2,32,16,128]{3,2,1,0:T(8,128)}), f32[2,32,16,128]{3,2,1,0:T(8,128)S(1)}, u32[]{:S(2)}, u32[]{:S(2)}) %all-to-all-start.2) | async-done | bytes 524320 | tf_op jit(solution)/shard_map/all_to_all | solution.py:334
  146.5 9.4 %all_to_all.25.i_ref = f32[2,32,16,128]{3,2,1,0:T(8,128)S(1)} all-to-all(f32[2,32,16,128]{3,2,1,0:T(8,128)S(1)} %spectrum.1), channel_id=1, replica_groups=mesh['dp'=2,'space'=16] {'dp'}, dimensions={0} | all-to-all | bytes 1048576 | tf_op jit(solution)/shard_map/all_to_all | solution.py:335
  155.8 6.3 %all-to-all-start.1 = ((f32[16,8,32,128]{3,2,1,0:T(8,128)}), f32[16,8,32,128]{3,2,1,0:T(8,128)S(1)}, u32[]{:S(2)}, u32[]{:S(2)}) async-start(f32[16,8,32,128]{3,2,1,0:T(8,128)} %copy-done.2), calls=%async_computation.1 | async-start | bytes 4194304 | tf_op jit(solution)/shard_map/all_to_all | solution.py:351
  162.2 0.8 copy.17
  163.0 2.6 broadcast_multiply_fusion
  165.6 4.7 %mul.33.k_ref = f32[256,256]{1,0:T(8,128)} reshape(f32[32,8,32,8]{3,2,1,0:T(8,128)} %broadcast_multiply_fusion) | data formatting | bytes 524288 | tf_op jit(solution)/shard_map/jit(kron)/mul | solution.py:353
  170.3 3.6 %reshape.23 = f32[32,8,32,8]{3,2,1,0:T(8,128)} reshape(f32[256,256]{1,0:T(8,128)S(1)} %get-tuple-element.14) | data formatting | bytes 524288 | tf_op jit(solution)/shard_map/reshape | solution.py:286
  173.9 2.7 select_reduce_fusion
  176.6 52.6 %psum.7 = f32[32,32]{1,0:T(8,128)} all-reduce(f32[32,32]{1,0:T(8,128)S(1)} %broadcast_multiply_fusion.1), channel_id=1, replica_groups=mesh['dp'=2,'space'=16] {'dp','space'}, use_global_device_ids=true, to_apply=%region_1.0 | all-reduce | flops 1024 | bytes 8192 | tf_op jit(solution)/shard_map/psum | solution.py:287
  229.1 0.9 copy-done.11
  230.0 8.2 %weight_grad.1 = f32[16,64,2048]{2,1,0:T(8,128)} custom-call(f32[2,32,16,128]{3,2,1,0:T(8,128)S(1)} %all-to-all-done.2.g_ref, f32[2,32,16,128]{3,2,1,0:T(8,128)S(1)} %all_to_all.25.i_ref, bf16[64,1024]{1,0:T(8,128)(2,1)S(1)} %copy-done.5, bf16[64,1024]{1,0:T(8,128)(2,1)S(1)} %copy-done.11), custom_call_target="tpu_custom_call" | custom-call | flops 1000000000 | bytes 8388608 | tf_op jit(solution)/shard_map/weight_grad/pallas_call | solution.py:337
  238.2 0.0 all-to-all-done.1.b_ref
  238.2 0.0 copy-done.6
  238.2 0.9 copy-done.15
  239.1 0.7 copy-done.16
  239.9 29.5 %inverse.1 = f32[1,32,8,128,128]{4,3,2,1,0:T(8,128)} custom-call(f32[16,8,32,128]{3,2,1,0:T(8,128)S(1)} %all-to-all-done.1.b_ref, f32[1,32,8,128,128]{4,3,2,1,0:T(8,128)} %get-tuple-element.11.gp_ref, f32[256,256]{1,0:T(8,128)S(1)} %copy-done.6, bf16[384,256]{1,0:T(8,128)(2,1)S(1)} %copy-done.15, bf16[96,128]{1,0:T(8,128)(2,1)S(1)} %copy-done.16), custom_call_target="tpu_custom_call" | custom-call | flops 10066329600 | bytes 33554432 | tf_op jit(solution)/shard_map/inverse/pallas_call | solution.py:354
  (10 shorter events, 0.0 us)
Async XLA Ops:
  0.6 0.9 copy-start.7
  1.6 0.7 copy-start.13
  26.9 1.3 copy-start.4
  28.2 6.7 %copy-start.8 = (bf16[768,128]{1,0:T(8,128)(2,1)S(1)}, bf16[768,128]{1,0:T(8,128)(2,1)}, u32[]{:S(2)}) copy-start(bf16[768,128]{1,0:T(8,128)(2,1)} %constant.22.clone.yf_ref) | copy-start | bytes 589828
  28.2 6.7 %copy-start.14 = (bf16[64,128]{1,0:T(8,128)(2,1)S(1)}, bf16[64,128]{1,0:T(8,128)(2,1)}, u32[]{:S(2)}) copy-start(bf16[64,128]{1,0:T(8,128)(2,1)} %constant.9.clone.zf_ref) | copy-start | bytes 49156
  28.2 54.1 %all-to-all-start = ((f32[16,8,32,128]{3,2,1,0:T(8,128)}), f32[16,8,32,128]{3,2,1,0:T(8,128)S(1)}, u32[]{:S(2)}, u32[]{:S(2)}) async-start(f32[16,8,32,128]{3,2,1,0:T(8,128)} %copy-done.4), calls=%async_computation | async-start | bytes 4194304 | tf_op jit(solution)/shard_map/all_to_all | solution.py:295
  69.0 1.3 copy-start.3
  70.3 18.2 %copy-start.5 = (bf16[64,1024]{1,0:T(8,128)(2,1)S(1)}, bf16[64,1024]{1,0:T(8,128)(2,1)}, u32[]{:S(2)}) copy-start(bf16[64,1024]{1,0:T(8,128)(2,1)} %constant.27.clone.eo_ref) | copy-start | bytes 393220
  70.3 18.2 %copy-start.9 = (bf16[64,384]{1,0:T(8,128)(2,1)S(1)}, bf16[64,384]{1,0:T(8,128)(2,1)}, u32[]{:S(2)}) copy-start(bf16[64,384]{1,0:T(8,128)(2,1)} %constant.23.clone.xf_ref) | copy-start | bytes 147460
  70.3 18.2 %copy-start.12 = (bf16[128,192]{1,0:T(8,128)(2,1)S(1)}, bf16[128,192]{1,0:T(8,128)(2,1)}, u32[]{:S(2)}) copy-start(bf16[128,192]{1,0:T(8,128)(2,1)} %constant.24.clone.xi_ref) | copy-start | bytes 147460
  82.3 1.3 copy-start
  83.6 52.3 %all-to-all-start.3 = ((f32[16,8,32,128]{3,2,1,0:T(8,128)}), f32[16,8,32,128]{3,2,1,0:T(8,128)S(1)}, u32[]{:S(2)}, u32[]{:S(2)}) async-start(f32[16,8,32,128]{3,2,1,0:T(8,128)} %copy-done.3), calls=%async_computation.3 | async-start | bytes 4194304 | tf_op jit(solution)/shard_map/all_to_all | solution.py:295
  88.6 1.6 copy-start.1
  105.9 1.3 copy-start.2
  135.9 10.5 %all-to-all-start.2 = ((f32[2,32,16,128]{3,2,1,0:T(8,128)}), f32[2,32,16,128]{3,2,1,0:T(8,128)S(1)}, u32[]{:S(2)}, u32[]{:S(2)}) async-start(f32[2,32,16,128]{3,2,1,0:T(8,128)} %get-tuple-element.12), calls=%async_computation.2 | async-start | bytes 1048576 | tf_op jit(solution)/shard_map/all_to_all | solution.py:334
  139.7 0.8 copy-start.10
  155.8 82.4 %all-to-all-start.1 = ((f32[16,8,32,128]{3,2,1,0:T(8,128)}), f32[16,8,32,128]{3,2,1,0:T(8,128)S(1)}, u32[]{:S(2)}, u32[]{:S(2)}) async-start(f32[16,8,32,128]{3,2,1,0:T(8,128)} %copy-done.2), calls=%async_computation.1 | async-start | bytes 4194304 | tf_op jit(solution)/shard_map/all_to_all | solution.py:351
  229.1 0.9 copy-start.11
  230.0 8.2 %copy-start.6 = (f32[256,256]{1,0:T(8,128)S(1)}, f32[256,256]{1,0:T(8,128)}, u32[]{:S(2)}) copy-start(f32[256,256]{1,0:T(8,128)} %mul.33.k_ref) | copy-start | bytes 786436
  238.2 0.9 copy-start.15
  239.1 0.7 copy-start.16

commit v2 on v1

--- a/solution.py
+++ b/solution.py
@@ -21,6 +21,7 @@
 BF = jnp.bfloat16
 F32 = jnp.float32
 LIMIT = 48 * 1024 * 1024
+FUSED_LIMIT = 60 * 1024 * 1024
 
 
 def signed(count):
@@ -135,6 +136,13 @@
         )
 
 
+def fold(x):
+    total = x[:, :128]
+    for t in range(1, C * C // 128):
+        total = total + x[:, t * 128 : (t + 1) * 128]
+    return total
+
+
 def swap(x):
     return pltpu.roll(x, MY, 1)
 
@@ -172,12 +180,6 @@
         g = tn(jnp.concatenate([hi, lo], 0), eo_ref[...])
         gr, gi = g[:MY], g[MY:]
         wr, wi = w_ref[u, :, : C * C], w_ref[u, :, C * C :]
-
-        def fold(x):
-            total = x[:, :128]
-            for t in range(1, C * C // 128):
-                total = total + x[:, t * 128 : (t + 1) * 128]
-            return total
 
         both = jnp.concatenate([fold(wr * gr + wi * gi), fold(wr * gi - wi * gr)], 0).T
         total = both[:C] + both[C : 2 * C] + both[2 * C : 3 * C] + both[3 * C :]
@@ -390,6 +392,301 @@
     return weight_grad, along.reshape(arrived_g.shape)
 
 
+def selector(rows):
+    row = lax.broadcasted_iota(jnp.int32, (rows, 8 * C), 0)
+    col = lax.broadcasted_iota(jnp.int32, (rows, 8 * C), 1)
+    return jnp.where(col // 8 == row, 1.0, 0.0).astype(BF)
+
+
+def same_row():
+    row = lax.broadcasted_iota(jnp.int32, (8 * C, 8 * C), 0)
+    col = lax.broadcasted_iota(jnp.int32, (8 * C, 8 * C), 1)
+    return row % 8 == col % 8
+
+
+def fused_kernel(
+    pre_ref, cot_ref, in_ref, w_ref, sw_ref, zf_ref, yf_ref, xf_ref, xi_ref, eo_ref,
+    skip_ref, spec_ref, sum_ref, back_ref,
+    gp_ref, k_ref, acc_ref, sg_ref, si_ref, sb_ref, rg_ref, ri_ref, d_ref, ss_ref, rs_ref,
+    send_g, send_i, send_b, send_s, recv_g, recv_i, recv_b, recv_s, local,
+    *, space, dp, xl, wstep,
+):
+    step = pl.program_id(0)
+    me = lax.axis_index("space")
+    half = lax.axis_index("dp")
+    mh = MX // dp
+    msteps = MX // wstep
+
+    def others(action):
+        @pl.loop(1, space)
+        def _(r):
+            action(lax.rem(me + r, space))
+
+    def put(src, dst, send, recv, target):
+        pltpu.make_async_remote_copy(
+            src_ref=src, dst_ref=dst, send_sem=send, recv_sem=recv,
+            device_id={"space": target}, device_id_type=pl.DeviceIdType.MESH,
+        ).start()
+
+    def await_all(ref, sem):
+        part = ref.at[pl.ds(0, space - 1)]
+        pltpu.make_async_copy(part, part, sem).wait()
+
+    @pl.when(step == 0)
+    def _():
+        barrier = pltpu.get_barrier_semaphore()
+
+        def greet(target):
+            pl.semaphore_signal(
+                barrier, inc=1, device_id={"space": target}, device_id_type=pl.DeviceIdType.MESH
+            )
+
+        others(greet)
+        pl.semaphore_wait(barrier, space - 1)
+        acc_ref[...] = jnp.zeros_like(acc_ref)
+        sel = selector(C)
+        pieces = []
+        for piece in split(sw_ref[...]):
+            wide = tn(piece, sel).astype(BF)
+            pieces.append(jnp.where(same_row(), tn(sel, wide), 0.0).astype(BF))
+        k_ref[...] = jnp.concatenate([pieces[0], pieces[1], pieces[0]], 1)
+
+    @pl.when(step < xl)
+    def _():
+        x = step
+        out2d = sg_ref.at[x].reshape(MZ * C, 2 * MY)
+        for g in range(0, C, GROUP):
+            gp = cot_ref[0, g : g + GROUP, 0] * gelu_slope(pre_ref[0, g : g + GROUP, 0])
+            gp_ref[x, g : g + GROUP] = gp
+            planes_forward(gp, g, zf_ref, yf_ref, out2d)
+        rg_ref[me, x] = sg_ref[x, me]
+        others(lambda t: put(sg_ref.at[x, t], rg_ref.at[me, x], send_g, recv_g, t))
+
+    @pl.when((step >= xl) & (step < 2 * xl))
+    def _():
+        x = step - xl
+        out2d = si_ref.at[x].reshape(MZ * C, 2 * MY)
+        for g in range(0, C, GROUP):
+            planes_forward(in_ref[0, g : g + GROUP, 0], g, zf_ref, yf_ref, out2d)
+        ri_ref[me, x] = si_ref[x, me]
+        others(lambda t: put(si_ref.at[x, t], ri_ref.at[me, x], send_i, recv_i, t))
+
+        @pl.loop(0, N // 16)
+        def _(s):
+            y = pl.multiple_of(s * 16, 16)
+            ga = gp_ref[x, :, pl.ds(y, 8), :].reshape(C * 8, N)
+            gb = gp_ref[x, :, pl.ds(y + 8, 8), :].reshape(C * 8, N)
+            gh, gl = split(jnp.concatenate([ga, gb], 1))
+            ia = in_ref[0, :, 0, pl.ds(y, 8), :].reshape(C * 8, N)
+            ib = in_ref[0, :, 0, pl.ds(y + 8, 8), :].reshape(C * 8, N)
+            ih, il = split(jnp.concatenate([ia, ib], 1))
+            acc_ref[...] += nt(
+                jnp.concatenate([gh, gl, gh], 1), jnp.concatenate([ih, ih, il], 1)
+            )
+            r = nn(k_ref[...], jnp.concatenate([gh, gh, gl], 0))
+            skip_ref[0, :, 0, pl.ds(y, 8), :] = r[:, :N].reshape(C, 8, N)
+            skip_ref[0, :, 0, pl.ds(y + 8, 8), :] = r[:, N:].reshape(C, 8, N)
+
+    @pl.when(step == 2 * xl - 1)
+    def _():
+        hi, lo = split(jnp.where(same_row(), acc_ref[...], 0.0))
+        sel = selector(C)
+        hi, lo = split(nn(sel, hi) + nn(sel, lo))
+        wide = selector(128)
+        ss_ref[...] = nt(hi, wide) + nt(lo, wide)
+        rs_ref[me] = ss_ref[...]
+        others(lambda t: put(ss_ref, rs_ref.at[me], send_s, recv_s, t))
+
+    s2d = spec_ref.reshape(dp * 2 * C * mh, 2 * MY)
+
+    @pl.when(step == 2 * xl)
+    def _():
+        await_all(rg_ref, recv_g)
+        await_all(rg_ref, send_g)
+        for c, s in x_forward(rg_ref.reshape(N * C, 2 * MY), xf_ref):
+            for h in range(dp):
+                spec_ref[lax.rem(h + half, dp), 0, c] = s[h * mh : (h + 1) * mh]
+
+    @pl.when(step >= 2 * xl)
+    def _():
+        for u in range(wstep):
+            m = (step - 2 * xl) * wstep + u
+            slot = lax.rem(m // mh + half, dp)
+            start = slot * (2 * C * mh) + lax.rem(m, mh)
+            hi, lo = split(s2d[pl.ds(start, C, stride=mh), :])
+            g = tn(jnp.concatenate([hi, lo], 0), eo_ref[...])
+            gr, gi = g[:MY], g[MY:]
+            wr, wi = w_ref[u, :, : C * C], w_ref[u, :, C * C :]
+            both = jnp.concatenate([fold(wr * gr + wi * gi), fold(wr * gi - wi * gr)], 0).T
+            total = both[:C] + both[C : 2 * C] + both[2 * C : 3 * C] + both[3 * C :]
+            d_ref[pl.ds(m, C, stride=MX), :] = total * NORM
+
+    @pl.when(step == 2 * xl + msteps - 1)
+    def _():
+        out2d = sb_ref.reshape(N * C, 2 * MY)
+        for i in range(C):
+            d = d_ref[i * MX : (i + 1) * MX, :]
+            hi, lo = split(jnp.concatenate([d, lane_sign(MX, -1.0) * swap(d)], 0))
+            out2d[pl.ds(i, N, stride=C), :] = nn(xi_ref[...], jnp.concatenate([hi, hi, lo], 0))
+        own = pltpu.make_async_copy(sb_ref.at[me], back_ref.at[me], local)
+        own.start()
+        others(lambda t: put(sb_ref.at[t], back_ref.at[me], send_b, recv_b, t))
+        await_all(rs_ref, recv_s)
+        await_all(rs_ref, send_s)
+        total = rs_ref[0]
+        for r in range(1, space):
+            total = total + rs_ref[r]
+        sum_ref[...] = total
+        await_all(ri_ref, recv_i)
+        await_all(ri_ref, send_i)
+        for c, s in x_forward(ri_ref.reshape(N * C, 2 * MY), xf_ref):
+            for h in range(dp):
+                spec_ref[lax.rem(h + half, dp), 1, c] = s[h * mh : (h + 1) * mh]
+        own.wait()
+        await_all(sb_ref, send_b)
+        await_all(sb_ref, recv_b)
+
+
+def pair_weight_kernel(mine_ref, other_ref, eo_ref, ei_ref, out_ref, *, step):
+    rows = mine_ref.shape[1] * mine_ref.shape[2] * mine_ref.shape[3]
+    mh = mine_ref.shape[3]
+    half = rows // 2
+    for u in range(step):
+        m = pl.program_id(0) * step + u
+        real = imag = None
+        for ref in (mine_ref, other_ref):
+            flat = ref.reshape(rows, 2 * MY)
+            gs = flat[pl.ds(m, C, stride=mh), :]
+            vs = flat[pl.ds(half + m, C, stride=mh), :]
+            g = tn(jnp.concatenate(split(gs), 0), eo_ref[...])
+            i = tn(jnp.concatenate(split(vs), 0), ei_ref[...])
+            gr, gi, ir, ii = g[:MY], g[MY:], i[:MY], i[MY:]
+            r = gr * ir + gi * ii
+            j = gi * ir - gr * ii
+            real, imag = (r, j) if real is None else (real + r, imag + j)
+        out_ref[u, :, : C * C] = real
+        out_ref[u, :, C * C :] = imag
+
+
+def restore_kernel(b_ref, sk_ref, yi_ref, zi_ref, out_ref, re_ref, im_ref):
+    hi, lo = split(b_ref.reshape(MZ * C, 2 * MY)[...])
+    v = nn(jnp.concatenate([hi, lo, hi], 1), yi_ref[...])
+    re_ref[...] = v[:, :N]
+    im_ref[...] = v[:, N:]
+    for i in range(C):
+        at = pl.ds(i, MZ, stride=C)
+        hi, lo = split(jnp.concatenate([re_ref[at, :], im_ref[at, :]], 0))
+        out_ref[0, i, 0] = sk_ref[0, i, 0] + tn(jnp.concatenate([hi, lo, hi], 0), zi_ref[...])
+
+
+def fused_body(space, dp, inputs, preact, cotangent, spectral_weight, skip_weight):
+    t = {k: jnp.asarray(v) for k, v in make_tables().items()}
+    xl = inputs.shape[2]
+    kl = spectral_weight.shape[1]
+    mh = MX // dp
+    field = jax.ShapeDtypeStruct(inputs.shape, F32)
+    wstep = 4
+    last = MX // wstep - 1
+    nbytes = inputs.size * 4
+
+    def plane(first):
+        return pl.BlockSpec((1, C, 1, N, N), lambda s: (0, 0, jnp.clip(s - first, 0, xl - 1), 0, 0))
+
+    arrive = (space, xl, C, 2 * MY)
+    send = (xl, space, C, 2 * MY)
+    spec_shape = (dp, 2, C, mh, 2 * MY)
+    dma = pltpu.SemaphoreType.DMA
+    skip_term, spec, summed, back = pl.pallas_call(
+        functools.partial(fused_kernel, space=space, dp=dp, xl=xl, wstep=wstep),
+        grid=(2 * xl + MX // wstep,),
+        in_specs=[
+            plane(0),
+            plane(0),
+            plane(xl),
+            pl.BlockSpec(
+                (wstep, kl, 2 * C * C), lambda s: (jnp.clip(s - 2 * xl, 0, last), 0, 0)
+            ),
+            whole(skip_weight.shape),
+            whole(t["zf"].shape),
+            whole(t["yf"].shape),
+            whole(t["xf"].shape),
+            whole(t["xi"].shape),
+            whole(t["eo"].shape),
+        ],
+        out_specs=[
+            plane(xl),
+            whole(spec_shape),
+            whole((C, 128)),
+            pl.BlockSpec(memory_space=pl.ANY),
+        ],
+        out_shape=[
+            field,
+            jax.ShapeDtypeStruct(spec_shape, F32),
+            jax.ShapeDtypeStruct((C, 128), F32),
+            jax.ShapeDtypeStruct(arrive, F32),
+        ],
+        scratch_shapes=[
+            pltpu.VMEM((xl, C, N, N), F32),
+            pltpu.VMEM((8 * C, 24 * C), BF),
+            pltpu.VMEM((8 * C, 8 * C), F32),
+            pltpu.VMEM(send, F32),
+            pltpu.VMEM(send, F32),
+            pltpu.VMEM(arrive, F32),
+            pltpu.VMEM(arrive, F32),
+            pltpu.VMEM(arrive, F32),
+            pltpu.VMEM((C * MX, 2 * MY), F32),
+            pltpu.VMEM((C, 128), F32),
+            pltpu.VMEM((space, C, 128), F32),
+        ]
+        + [dma] * 9,
+        compiler_params=pltpu.CompilerParams(
+            vmem_limit_bytes=FUSED_LIMIT, collective_id=0, has_side_effects=True
+        ),
+        cost_estimate=cost(nbytes * 1500, nbytes * 5),
+        name="fused_forward",
+    )(
+        preact, cotangent, inputs, spectral_weight, skip_weight,
+        t["zf"], t["yf"], t["xf"], t["xi"], t["eo"],
+    )
+    pairs = [(0, 1), (1, 0)]
+    theirs = lax.ppermute(spec[1:], "dp", pairs)
+    skip_grad = NORM * (summed + lax.ppermute(summed, "dp", pairs))[:, :C]
+    input_grad = pl.pallas_call(
+        restore_kernel,
+        grid=(xl,),
+        in_specs=[
+            pl.BlockSpec((MZ, 1, C, 2 * MY), lambda x: (0, x, 0, 0)),
+            pl.BlockSpec((1, C, 1, N, N), lambda x: (0, 0, x, 0, 0)),
+            whole(t["yi"].shape),
+            whole(t["zi"].shape),
+        ],
+        out_specs=pl.BlockSpec((1, C, 1, N, N), lambda x: (0, 0, x, 0, 0)),
+        out_shape=field,
+        scratch_shapes=[pltpu.VMEM((MZ * C, N), F32)] * 2,
+        compiler_params=params(),
+        cost_estimate=cost(nbytes * 300, nbytes * 2),
+        name="inverse",
+    )(back, skip_term, t["yi"], t["zi"])
+    step = 2
+    half_shape = (1,) + spec_shape[1:]
+    weight_grad = pl.pallas_call(
+        functools.partial(pair_weight_kernel, step=step),
+        grid=(mh // step,),
+        in_specs=[
+            whole(half_shape),
+            whole(half_shape),
+            whole(t["eo"].shape),
+            whole(t["ei"].shape),
+        ],
+        out_specs=pl.BlockSpec((step, kl, 2 * C * C), lambda m: (m, 0, 0)),
+        out_shape=jax.ShapeDtypeStruct((mh, kl, 2 * C * C), F32),
+        compiler_params=params(),
+        cost_estimate=cost(1e9, mh * kl * 2 * C * C * 4),
+        name="weight_grad",
+    )(spec[:1], theirs, t["eo"], t["ei"])
+    return input_grad, weight_grad, skip_grad
+
+
 def solution(mesh):
     in_specs = (
         P("dp", None, "space", None, None),
@@ -399,5 +696,7 @@
         P(),
     )
     out_specs = (P("dp", None, "space", None, None), P("dp", "space", None), P())
-    local = functools.partial(body, mesh.shape["space"], mesh.shape["dp"])
+    space, dp = mesh.shape["space"], mesh.shape["dp"]
+    form = fused_body if space == MZ and dp == 2 else body
+    local = functools.partial(form, space, dp)
     return jax.shard_map(local, mesh=mesh, in_specs=in_specs, out_specs=out_specs, check_vma=False)

time: 274 us -> 186 us (0.68); the launches traced: 269 us -> 185 us
  Pallas kernels: 115 us -> 180 us
  blocking collectives: 61.9 us -> 0 us
  waiting for transfers between devices: 44.3 us -> 0.01 us
  starting transfers between devices: 21.7 us -> 1.6 us
  local copies, waits for them, and re-layouts: 21 us -> 2.89 us
  other arithmetic: 5.32 us -> 0.61 us
    pallas_call x6 -> x3, Pallas kernels: 115 us -> 180 us  [the longest x1 154 us: fused_body(): pl.pallas_call(functools.partial(fused_kernel, space=space, dp=dp, xl=xl,...]
    psum x1 -> x0, blocking collectives: 52.6 us -> none  [body(): skip_grad = lax.psum(NORM * diag, ('dp', 'space'))]
    all_to_all x4 -> x0, waiting for transfers between devices: 44.3 us -> none  [the longest x2 40.7 us: outward(): return lax.all_to_all(p, 'space', split_axis=0, concat_axis=0, tiled=True)]
    all_to_all x4 -> x0, starting transfers between devices: 21.7 us -> none  [the longest x2 11.6 us: outward(): return lax.all_to_all(p, 'space', split_axis=0, concat_axis=0, tiled=True)]
    unnamed x34 -> x12, local copies, waits for them, and re-layouts: 11.9 us -> 1.62 us
    all_to_all x1 -> x0, blocking collectives: 9.39 us -> none  [body(): lax.all_to_all(spec_i, 'dp', split_axis=0, concat_axis=0, tiled=True)]
    mul x1 -> x0, local copies, waits for them, and re-layouts: 4.68 us -> none  [body(): kron = jnp.kron(skip_weight.T, jnp.eye(8, dtype=F32))]
    reshape x1 -> x0, local copies, waits for them, and re-layouts: 3.61 us -> none  [body(): acc.reshape(C, 8, C, 8)]
  transfers between devices with their start and end apart: 4 -> 2, of which waited for: 3 -> 0; matrix products, arithmetic and copies ran while one was open for 5% -> 1% of each run, Pallas kernels for 22% -> 9%
where the time goes in v2:
time: 186 us; the launch traced here: 185 us
  Pallas kernels  180 us (97%)
  local copies, waits for them, and re-layouts  2.89 us (2%)
    pallas_call x1, Pallas kernels, fused_body(): pl.pallas_call(functools.partial(fused_kernel, space=space, dp=dp, xl=xl,...  154 us
    pallas_call x1, Pallas kernels, fused_body(): pl.pallas_call(restore_kernel, grid=(xl,), in_specs=[pl.BlockSpec((MZ, 1,...  17.6 us
    pallas_call x1, Pallas kernels, fused_body(): pl.pallas_call(functools.partial(pair_weight_kernel, step=step), grid=(mh...  8.18 us
  transfers between devices with their start and end apart: 2, of which 0 were waited for; matrix products, arithmetic and copies ran while one was open for 1% of the time, Pallas kernels for 9%

profile of v2, /device:TPU:15, one launch (start us, length us, event | category | flops | bytes accessed | tf_op | source)
XLA Modules:
  0.0 185.4 jit_solution(12998752602444431679)
XLA Ops:
  0.6 0.0 copy-start.1
  0.6 0.0 copy-start.4
  0.7 153.8 %fused_forward.1 = (f32[1,32,8,128,128]{4,3,2,1,0:T(8,128)}, f32[2,2,32,16,128]{4,3,2,1,0:T(8,128)}, f32[32,128]{1,0:T(8,128)}, f32[16,8,32,128]{3,2,1,0:T(8,128)}) custom-call(f32[1,32,8,128,128]{4,3,2,1,0:T(8,128)} %pre_ref.1, f32[1,32,8,128,128]{4,3,2,1,0:T(8,128)} %cot_ref.1, f32[1,32,8,128,128]{4,3,2,1,0:T(8,128)} %in_ref.1, f32[32,64,2048]{2,1,0:T(8,128)} %w_ref.1, ...), custom_call_target="tpu_custom_call" | custom-call | flops 25165824000 | bytes 83886080 | tf_op jit(solution)/shard_map/fused_forward/pallas_call | solution.py:599
  154.5 0.3 collective-permute-start.1
  154.8 1.3 fusion.1
  156.1 1.3 collective-permute-start
  157.4 0.0 copy-done.1
  157.4 0.0 copy-done.4
  157.4 0.0 copy-start
  157.4 1.6 copy-done
  159.0 0.0 copy-start.5
  159.0 0.0 copy-start.2
  159.0 0.0 copy-start.3
  159.0 17.6 %inverse.1 = f32[1,32,8,128,128]{4,3,2,1,0:T(8,128)} custom-call(f32[16,8,32,128]{3,2,1,0:T(8,128)S(1)} %copy-done, f32[1,32,8,128,128]{4,3,2,1,0:T(8,128)} %get-tuple-element.8.sk_ref, bf16[384,256]{1,0:T(8,128)(2,1)S(1)} %copy-done.1, bf16[96,128]{1,0:T(8,128)(2,1)S(1)} %copy-done.4), custom_call_target="tpu_custom_call" | custom-call | flops 5033164800 | bytes 33554432 | tf_op jit(solution)/shard_map/inverse/pallas_call | solution.py:654
  176.6 0.0 collective-permute-done.1
  176.6 0.0 copy-done.5
  176.6 0.6 fusion
  177.2 0.0 collective-permute-done.other_ref
  177.2 0.0 copy-done.2
  177.2 0.0 copy-done.3
  177.2 8.2 %weight_grad.1 = f32[16,64,2048]{2,1,0:T(8,128)} custom-call(f32[1,2,32,16,128]{4,3,2,1,0:T(8,128)S(1)} %get-tuple-element.12.mine_ref, f32[1,2,32,16,128]{4,3,2,1,0:T(8,128)S(1)} %collective-permute-done.other_ref, bf16[64,1024]{1,0:T(8,128)(2,1)S(1)} %copy-done.2, bf16[64,1024]{1,0:T(8,128)(2,1)S(1)} %copy-done.3), custom_call_target="tpu_custom_call" | custom-call | flops 1000000000 | bytes 8388608 | tf_op jit(solution)/shard_map/weight_grad/pallas_call | solution.py:672
Async XLA Ops:
  0.6 156.8 %copy-start.1 = (bf16[384,256]{1,0:T(8,128)(2,1)S(1)}, bf16[384,256]{1,0:T(8,128)(2,1)}, u32[]{:S(2)}) copy-start(bf16[384,256]{1,0:T(8,128)(2,1)} %constant.22.clone.yi_ref) | copy-start | bytes 589828
  0.6 156.7 %copy-start.4 = (bf16[96,128]{1,0:T(8,128)(2,1)S(1)}, bf16[96,128]{1,0:T(8,128)(2,1)}, u32[]{:S(2)}) copy-start(bf16[96,128]{1,0:T(8,128)(2,1)} %constant.23.clone.zi_ref) | copy-start | bytes 73732
  154.5 22.1 %collective-permute-start.1 = (f32[32,128]{1,0:T(8,128)}, f32[32,128]{1,0:T(8,128)S(1)}, u32[]{:S(2)}, u32[]{:S(2)}) collective-permute-start(f32[32,128]{1,0:T(8,128)} %get-tuple-element.10), channel_id=1, source_target_pairs={{0,16},{16,0},{1,17},{17,1},{2,18},{18,2},{3,19},{19,3},{4,20},{20... | collective-permute-start | bytes 49160 | tf_op jit(solution)/shard_map/ppermute | solution.py:653
  156.1 21.1 %collective-permute-start = (f32[1,2,32,16,128]{4,3,2,1,0:T(8,128)S(1)}, f32[1,2,32,16,128]{4,3,2,1,0:T(8,128)S(1)}, u32[]{:S(2)}, u32[]{:S(2)}) collective-permute-start(f32[1,2,32,16,128]{4,3,2,1,0:T(8,128)S(1)} %get-tuple-element.11), channel_id=1, source_target_pairs={{0,16},{16,0},{1,17},{17,1},{2,18},{18,2},{3,19},{19,3},{4,20},{20... | collective-permute-start | bytes 1572872 | tf_op jit(solution)/shard_map/ppermute | solution.py:652
  157.4 1.6 copy-start
  159.0 17.6 %copy-start.5 = (f32[32,128]{1,0:T(8,128)S(1)}, f32[32,128]{1,0:T(8,128)}, u32[]{:S(2)}) copy-start(f32[32,128]{1,0:T(8,128)} %get-tuple-element.10) | copy-start | bytes 49156
  159.0 18.2 %copy-start.2 = (bf16[64,1024]{1,0:T(8,128)(2,1)S(1)}, bf16[64,1024]{1,0:T(8,128)(2,1)}, u32[]{:S(2)}) copy-start(bf16[64,1024]{1,0:T(8,128)(2,1)} %constant.24.clone.eo_ref) | copy-start | bytes 393220
  159.0 18.2 %copy-start.3 = (bf16[64,1024]{1,0:T(8,128)(2,1)S(1)}, bf16[64,1024]{1,0:T(8,128)(2,1)}, u32[]{:S(2)}) copy-start(bf16[64,1024]{1,0:T(8,128)(2,1)} %constant.25.clone.ei_ref) | copy-start | bytes 393220

commit v3 on v2

--- a/solution.py
+++ b/solution.py
@@ -55,6 +55,8 @@
     t["yi"] = np.concatenate([hi, hi, lo], 0)
     hi, lo = halves(np.concatenate([cz, -sz], 0))
     t["zi"] = np.concatenate([hi, hi, lo], 0)
+    four = [np.kron(np.eye(4), p.astype(np.float32)).astype(ml_dtypes.bfloat16) for p in (hi, lo)]
+    t["zi4"] = np.concatenate([four[0], four[0], four[1]], 0)
     eye = np.eye(C)
     spread_out = np.repeat(eye, C, axis=1)
     spread_in = np.tile(eye, (1, C))
@@ -406,9 +408,9 @@
 
 def fused_kernel(
     pre_ref, cot_ref, in_ref, w_ref, sw_ref, zf_ref, yf_ref, xf_ref, xi_ref, eo_ref,
-    skip_ref, spec_ref, sum_ref, back_ref,
-    gp_ref, k_ref, acc_ref, sg_ref, si_ref, sb_ref, rg_ref, ri_ref, d_ref, ss_ref, rs_ref,
-    send_g, send_i, send_b, send_s, recv_g, recv_i, recv_b, recv_s, local,
+    skip_ref, mine_ref, theirs_ref, sum_ref, along_ref,
+    gp_ref, k_ref, acc_ref, sg_ref, si_ref, spec_ref, rg_ref, ri_ref, d_ref, ss_ref, rs_ref,
+    send_g, send_i, send_s, recv_g, recv_i, recv_s,
     *, space, dp, xl, wstep,
 ):
     step = pl.program_id(0)
@@ -523,14 +525,11 @@
 
     @pl.when(step == 2 * xl + msteps - 1)
     def _():
-        out2d = sb_ref.reshape(N * C, 2 * MY)
+        out2d = along_ref.reshape(N * C, 2 * MY)
         for i in range(C):
             d = d_ref[i * MX : (i + 1) * MX, :]
             hi, lo = split(jnp.concatenate([d, lane_sign(MX, -1.0) * swap(d)], 0))
             out2d[pl.ds(i, N, stride=C), :] = nn(xi_ref[...], jnp.concatenate([hi, hi, lo], 0))
-        own = pltpu.make_async_copy(sb_ref.at[me], back_ref.at[me], local)
-        own.start()
-        others(lambda t: put(sb_ref.at[t], back_ref.at[me], send_b, recv_b, t))
         await_all(rs_ref, recv_s)
         await_all(rs_ref, send_s)
         total = rs_ref[0]
@@ -542,14 +541,13 @@
         for c, s in x_forward(ri_ref.reshape(N * C, 2 * MY), xf_ref):
             for h in range(dp):
                 spec_ref[lax.rem(h + half, dp), 1, c] = s[h * mh : (h + 1) * mh]
-        own.wait()
-        await_all(sb_ref, send_b)
-        await_all(sb_ref, recv_b)
+        mine_ref[...] = spec_ref[0]
+        theirs_ref[...] = spec_ref[1]
 
 
 def pair_weight_kernel(mine_ref, other_ref, eo_ref, ei_ref, out_ref, *, step):
-    rows = mine_ref.shape[1] * mine_ref.shape[2] * mine_ref.shape[3]
-    mh = mine_ref.shape[3]
+    mh = mine_ref.shape[2]
+    rows = 2 * C * mh
     half = rows // 2
     for u in range(step):
         m = pl.program_id(0) * step + u
@@ -573,10 +571,20 @@
     v = nn(jnp.concatenate([hi, lo, hi], 1), yi_ref[...])
     re_ref[...] = v[:, :N]
     im_ref[...] = v[:, N:]
-    for i in range(C):
-        at = pl.ds(i, MZ, stride=C)
-        hi, lo = split(jnp.concatenate([re_ref[at, :], im_ref[at, :]], 0))
-        out_ref[0, i, 0] = sk_ref[0, i, 0] + tn(jnp.concatenate([hi, lo, hi], 0), zi_ref[...])
+    for first in range(0, C, 16):
+        turned = []
+        for q in range(first, first + 16, 4):
+            pieces = []
+            for i in range(q, q + 4):
+                at = pl.ds(i, MZ, stride=C)
+                pieces += [re_ref[at, :], im_ref[at, :]]
+            turned.append(jnp.concatenate(pieces, 0).T)
+        hi, lo = split(jnp.concatenate(turned, 0))
+        r = nn(jnp.concatenate([hi, lo, hi], 1), zi_ref[...])
+        for k in range(16):
+            rows = slice(k // 4 * N, (k // 4 + 1) * N)
+            cols = slice(k % 4 * N, (k % 4 + 1) * N)
+            out_ref[0, first + k, 0] = sk_ref[0, first + k, 0] + r[rows, cols]
 
 
 def fused_body(space, dp, inputs, preact, cotangent, spectral_weight, skip_weight):
@@ -594,9 +602,10 @@
 
     arrive = (space, xl, C, 2 * MY)
     send = (xl, space, C, 2 * MY)
-    spec_shape = (dp, 2, C, mh, 2 * MY)
+    half_shape = (2, C, mh, 2 * MY)
+    spec_shape = (dp,) + half_shape
     dma = pltpu.SemaphoreType.DMA
-    skip_term, spec, summed, back = pl.pallas_call(
+    skip_term, mine, send_half, summed, along = pl.pallas_call(
         functools.partial(fused_kernel, space=space, dp=dp, xl=xl, wstep=wstep),
         grid=(2 * xl + MX // wstep,),
         in_specs=[
@@ -615,13 +624,15 @@
         ],
         out_specs=[
             plane(xl),
-            whole(spec_shape),
+            whole(half_shape),
+            whole(half_shape),
             whole((C, 128)),
-            pl.BlockSpec(memory_space=pl.ANY),
+            whole(arrive),
         ],
         out_shape=[
             field,
-            jax.ShapeDtypeStruct(spec_shape, F32),
+            jax.ShapeDtypeStruct(half_shape, F32),
+            jax.ShapeDtypeStruct(half_shape, F32),
             jax.ShapeDtypeStruct((C, 128), F32),
             jax.ShapeDtypeStruct(arrive, F32),
         ],
@@ -631,14 +642,14 @@
             pltpu.VMEM((8 * C, 8 * C), F32),
             pltpu.VMEM(send, F32),
             pltpu.VMEM(send, F32),
-            pltpu.VMEM(arrive, F32),
+            pltpu.VMEM(spec_shape, F32),
             pltpu.VMEM(arrive, F32),
             pltpu.VMEM(arrive, F32),
             pltpu.VMEM((C * MX, 2 * MY), F32),
             pltpu.VMEM((C, 128), F32),
             pltpu.VMEM((space, C, 128), F32),
         ]
-        + [dma] * 9,
+        + [dma] * 6,
         compiler_params=pltpu.CompilerParams(
             vmem_limit_bytes=FUSED_LIMIT, collective_id=0, has_side_effects=True
         ),
@@ -649,7 +660,8 @@
         t["zf"], t["yf"], t["xf"], t["xi"], t["eo"],
     )
     pairs = [(0, 1), (1, 0)]
-    theirs = lax.ppermute(spec[1:], "dp", pairs)
+    back = lax.all_to_all(along, "space", split_axis=0, concat_axis=0, tiled=True)
+    theirs = lax.ppermute(send_half, "dp", pairs)
     skip_grad = NORM * (summed + lax.ppermute(summed, "dp", pairs))[:, :C]
     input_grad = pl.pallas_call(
         restore_kernel,
@@ -658,7 +670,7 @@
             pl.BlockSpec((MZ, 1, C, 2 * MY), lambda x: (0, x, 0, 0)),
             pl.BlockSpec((1, C, 1, N, N), lambda x: (0, 0, x, 0, 0)),
             whole(t["yi"].shape),
-            whole(t["zi"].shape),
+            whole(t["zi4"].shape),
         ],
         out_specs=pl.BlockSpec((1, C, 1, N, N), lambda x: (0, 0, x, 0, 0)),
         out_shape=field,
@@ -666,9 +678,8 @@
         compiler_params=params(),
         cost_estimate=cost(nbytes * 300, nbytes * 2),
         name="inverse",
-    )(back, skip_term, t["yi"], t["zi"])
+    )(back, skip_term, t["yi"], t["zi4"])
     step = 2
-    half_shape = (1,) + spec_shape[1:]
     weight_grad = pl.pallas_call(
         functools.partial(pair_weight_kernel, step=step),
         grid=(mh // step,),
@@ -683,7 +694,7 @@
         compiler_params=params(),
         cost_estimate=cost(1e9, mh * kl * 2 * C * C * 4),
         name="weight_grad",
-    )(spec[:1], theirs, t["eo"], t["ei"])
+    )(mine, theirs, t["eo"], t["ei"])
     return input_grad, weight_grad, skip_grad
 
 

time: 186 us -> 185 us (level)
  Pallas kernels: 180 us -> 138 us
  waiting for transfers between devices: 0.01 us -> 35.4 us
  starting transfers between devices: 1.6 us -> 7.55 us
    pallas_call x1, Pallas kernels: 154 us -> 113 us  [fused_body(): pl.pallas_call(functools.partial(fused_kernel, space=space, dp=dp, xl=xl,...]
    all_to_all x0 -> x1, waiting for transfers between devices: none -> 23.2 us  [fused_body(): lax.all_to_all(along, 'space', split_axis=0, concat_axis=0, tiled=True)]
    ppermute x1, waiting for transfers between devices: 0.01 us -> 12.2 us  [fused_body(): skip_grad = NORM * (summed + lax.ppermute(summed, 'dp', pairs))[:, :C]]
    all_to_all x0 -> x1, starting transfers between devices: none -> 6.08 us  [fused_body(): lax.all_to_all(along, 'space', split_axis=0, concat_axis=0, tiled=True)]
  transfers between devices with their start and end apart: 2 -> 3, of which waited for: 0 -> 2; matrix products, arithmetic and copies ran while one was open for 1% -> 1% of each run, Pallas kernels for 9% -> 4%
where the time goes in v3:
time: 185 us; the launch traced here: 184 us
  Pallas kernels  138 us (75%)
  waiting for transfers between devices  35.4 us (19%)
  starting transfers between devices  7.55 us (4%)
    pallas_call x1, Pallas kernels, fused_body(): pl.pallas_call(functools.partial(fused_kernel, space=space, dp=dp, xl=xl,...  113 us
    all_to_all x1, waiting for transfers between devices, fused_body(): lax.all_to_all(along, 'space', split_axis=0, concat_axis=0, tiled=True)  23.2 us
    pallas_call x1, Pallas kernels, fused_body(): pl.pallas_call(restore_kernel, grid=(xl,), in_specs=[pl.BlockSpec((MZ, 1,...  17.4 us
    ppermute x1, waiting for transfers between devices, fused_body(): skip_grad = NORM * (summed + lax.ppermute(summed, 'dp', pairs))[:, :C]  12.2 us
    pallas_call x1, Pallas kernels, fused_body(): pl.pallas_call(functools.partial(pair_weight_kernel, step=step), grid=(mh...  8.16 us
    all_to_all x1, starting transfers between devices, fused_body(): lax.all_to_all(along, 'space', split_axis=0, concat_axis=0, tiled=True)  6.08 us
  transfers between devices with their start and end apart: 3, of which 2 were waited for; matrix products, arithmetic and copies ran while one was open for 1% of the time, Pallas kernels for 4%

profile of v3, /device:TPU:15, one launch (start us, length us, event | category | flops | bytes accessed | tf_op | source)
XLA Modules:
  0.0 184.3 jit_solution(2244448978570481923)
XLA Ops:
  0.6 0.0 copy-start.3
  0.6 0.0 copy-start.4
  0.7 0.0 copy-start.1
  0.7 0.0 copy-start.2
  0.7 112.8 %fused_forward.1 = (f32[1,32,8,128,128]{4,3,2,1,0:T(8,128)}, f32[2,32,16,128]{3,2,1,0:T(8,128)}, f32[2,32,16,128]{3,2,1,0:T(8,128)}, f32[32,128]{1,0:T(8,128)}, f32[16,8,32,128]{3,2,1,0:T(8,128)}) custom-call(f32[1,32,8,128,128]{4,3,2,1,0:T(8,128)} %pre_ref.1, f32[1,32,8,128,128]{4,3,2,1,0:T(8,128)} %cot_ref.1, f32[1,32,8,128,128]{4,3,2,1,0:T(8,128)} %in_ref.1, ...), custom_call_target="tpu_custom_call" | custom-call | flops 25165824000 | bytes 83886080 | tf_op jit(solution)/shard_map/fused_forward/pallas_call | solution.py:608
  113.4 6.1 %all-to-all-start = ((f32[16,8,32,128]{3,2,1,0:T(8,128)}), f32[16,8,32,128]{3,2,1,0:T(8,128)S(1)}, u32[]{:S(2)}, u32[]{:S(2)}) async-start(f32[16,8,32,128]{3,2,1,0:T(8,128)} %get-tuple-element.8), calls=%async_computation | async-start | bytes 4194304 | tf_op jit(solution)/shard_map/all_to_all | solution.py:663
  119.5 0.3 collective-permute-start
  119.8 1.2 collective-permute-start.1
  121.0 12.2 %collective-permute-done.1 = f32[32,128]{1,0:T(8,128)S(1)} collective-permute-done((f32[32,128]{1,0:T(8,128)}, f32[32,128]{1,0:T(8,128)S(1)}, u32[]{:S(2)}, u32[]{:S(2)}) %collective-permute-start.1) | collective-permute-done | bytes 16416 | tf_op jit(solution)/shard_map/ppermute | solution.py:665
  133.2 1.3 fusion
  134.6 0.0 collective-permute-done.other_ref
  134.6 0.0 copy-done.3
  134.6 0.0 copy-done.4
  134.6 0.0 copy-start
  134.6 1.0 copy-done
  135.6 8.2 %weight_grad.1 = f32[16,64,2048]{2,1,0:T(8,128)} custom-call(f32[2,32,16,128]{3,2,1,0:T(8,128)S(1)} %copy-done, f32[2,32,16,128]{3,2,1,0:T(8,128)S(1)} %collective-permute-done.other_ref, bf16[64,1024]{1,0:T(8,128)(2,1)S(1)} %copy-done.3, bf16[64,1024]{1,0:T(8,128)(2,1)S(1)} %copy-done.4), custom_call_target="tpu_custom_call" | custom-call | flops 1000000000 | bytes 8388608 | tf_op jit(solution)/shard_map/weight_grad/pallas_call | solution.py:683
  143.8 23.2 %all-to-all-done.b_ref = f32[16,8,32,128]{3,2,1,0:T(8,128)S(1)} async-done(((f32[16,8,32,128]{3,2,1,0:T(8,128)}), f32[16,8,32,128]{3,2,1,0:T(8,128)S(1)}, u32[]{:S(2)}, u32[]{:S(2)}) %all-to-all-start) | async-done | bytes 2097184 | tf_op jit(solution)/shard_map/all_to_all | solution.py:663
  166.9 0.0 copy-done.1
  166.9 0.0 copy-done.2
  166.9 17.4 %inverse.1 = f32[1,32,8,128,128]{4,3,2,1,0:T(8,128)} custom-call(f32[16,8,32,128]{3,2,1,0:T(8,128)S(1)} %all-to-all-done.b_ref, f32[1,32,8,128,128]{4,3,2,1,0:T(8,128)} %get-tuple-element.9.sk_ref, bf16[384,256]{1,0:T(8,128)(2,1)S(1)} %copy-done.2, bf16[384,512]{1,0:T(8,128)(2,1)S(1)} %copy-done.1), custom_call_target="tpu_custom_call" | custom-call | flops 5033164800 | bytes 33554432 | tf_op jit(solution)/shard_map/inverse/pallas_call | solution.py:666
Async XLA Ops:
  0.6 133.9 %copy-start.3 = (bf16[64,1024]{1,0:T(8,128)(2,1)S(1)}, bf16[64,1024]{1,0:T(8,128)(2,1)}, u32[]{:S(2)}) copy-start(bf16[64,1024]{1,0:T(8,128)(2,1)} %constant.24.clone.eo_ref) | copy-start | bytes 393220
  0.6 133.9 %copy-start.4 = (bf16[64,1024]{1,0:T(8,128)(2,1)S(1)}, bf16[64,1024]{1,0:T(8,128)(2,1)}, u32[]{:S(2)}) copy-start(bf16[64,1024]{1,0:T(8,128)(2,1)} %constant.25.clone.ei_ref) | copy-start | bytes 393220
  0.7 166.3 %copy-start.1 = (bf16[384,512]{1,0:T(8,128)(2,1)S(1)}, bf16[384,512]{1,0:T(8,128)(2,1)}, u32[]{:S(2)}) copy-start(bf16[384,512]{1,0:T(8,128)(2,1)} %constant.23.clone.zi_ref) | copy-start | bytes 1179652
  0.7 166.3 %copy-start.2 = (bf16[384,256]{1,0:T(8,128)(2,1)S(1)}, bf16[384,256]{1,0:T(8,128)(2,1)}, u32[]{:S(2)}) copy-start(bf16[384,256]{1,0:T(8,128)(2,1)} %constant.22.clone.yi_ref) | copy-start | bytes 589828
  113.4 53.5 %all-to-all-start = ((f32[16,8,32,128]{3,2,1,0:T(8,128)}), f32[16,8,32,128]{3,2,1,0:T(8,128)S(1)}, u32[]{:S(2)}, u32[]{:S(2)}) async-start(f32[16,8,32,128]{3,2,1,0:T(8,128)} %get-tuple-element.8), calls=%async_computation | async-start | bytes 4194304 | tf_op jit(solution)/shard_map/all_to_all | solution.py:663
  119.5 15.0 %collective-permute-start = (f32[2,32,16,128]{3,2,1,0:T(8,128)}, f32[2,32,16,128]{3,2,1,0:T(8,128)S(1)}, u32[]{:S(2)}, u32[]{:S(2)}) collective-permute-start(f32[2,32,16,128]{3,2,1,0:T(8,128)} %get-tuple-element.11), channel_id=1, source_target_pairs={{0,16},{16,0},{1,17},{17,1},{2,18},{18,2},{3,19},{19,3},{4,20},{20... | collective-permute-start | bytes 1572872 | tf_op jit(solution)/shard_map/ppermute | solution.py:664
  119.8 13.5 %collective-permute-start.1 = (f32[32,128]{1,0:T(8,128)}, f32[32,128]{1,0:T(8,128)S(1)}, u32[]{:S(2)}, u32[]{:S(2)}) collective-permute-start(f32[32,128]{1,0:T(8,128)} %get-tuple-element.12), channel_id=1, source_target_pairs={{0,16},{16,0},{1,17},{17,1},{2,18},{18,2},{3,19},{19,3},{4,20},{20... | collective-permute-start | bytes 49160 | tf_op jit(solution)/shard_map/ppermute | solution.py:665
  134.6 1.0 copy-start

commit v4 on v3

--- a/solution.py
+++ b/solution.py
@@ -408,9 +408,9 @@
 
 def fused_kernel(
     pre_ref, cot_ref, in_ref, w_ref, sw_ref, zf_ref, yf_ref, xf_ref, xi_ref, eo_ref,
-    skip_ref, mine_ref, theirs_ref, sum_ref, along_ref,
-    gp_ref, k_ref, acc_ref, sg_ref, si_ref, spec_ref, rg_ref, ri_ref, d_ref, ss_ref, rs_ref,
-    send_g, send_i, send_s, recv_g, recv_i, recv_s,
+    skip_ref, mine_ref, theirs_ref, sum_ref, back_ref,
+    gp_ref, k_ref, acc_ref, sg_ref, si_ref, sb_ref, spec_ref, rg_ref, ri_ref, d_ref, ss_ref, rs_ref,
+    send_g, send_i, send_b, send_s, recv_g, recv_i, recv_b, recv_s, local,
     *, space, dp, xl, wstep,
 ):
     step = pl.program_id(0)
@@ -472,6 +472,10 @@
             planes_forward(in_ref[0, g : g + GROUP, 0], g, zf_ref, yf_ref, out2d)
         ri_ref[me, x] = si_ref[x, me]
         others(lambda t: put(si_ref.at[x, t], ri_ref.at[me, x], send_i, recv_i, t))
+
+    @pl.when(step >= 2 * xl + msteps)
+    def _():
+        x = step - 2 * xl - msteps
 
         @pl.loop(0, N // 16)
         def _(s):
@@ -489,7 +493,7 @@
             skip_ref[0, :, 0, pl.ds(y, 8), :] = r[:, :N].reshape(C, 8, N)
             skip_ref[0, :, 0, pl.ds(y + 8, 8), :] = r[:, N:].reshape(C, 8, N)
 
-    @pl.when(step == 2 * xl - 1)
+    @pl.when(step == 3 * xl + msteps - 1)
     def _():
         hi, lo = split(jnp.where(same_row(), acc_ref[...], 0.0))
         sel = selector(C)
@@ -509,7 +513,7 @@
             for h in range(dp):
                 spec_ref[lax.rem(h + half, dp), 0, c] = s[h * mh : (h + 1) * mh]
 
-    @pl.when(step >= 2 * xl)
+    @pl.when((step >= 2 * xl) & (step < 2 * xl + msteps))
     def _():
         for u in range(wstep):
             m = (step - 2 * xl) * wstep + u
@@ -525,11 +529,16 @@
 
     @pl.when(step == 2 * xl + msteps - 1)
     def _():
-        out2d = along_ref.reshape(N * C, 2 * MY)
+        out2d = sb_ref.reshape(N * C, 2 * MY)
         for i in range(C):
             d = d_ref[i * MX : (i + 1) * MX, :]
             hi, lo = split(jnp.concatenate([d, lane_sign(MX, -1.0) * swap(d)], 0))
             out2d[pl.ds(i, N, stride=C), :] = nn(xi_ref[...], jnp.concatenate([hi, hi, lo], 0))
+        pltpu.make_async_copy(sb_ref.at[me], back_ref.at[me], local).start()
+        others(lambda t: put(sb_ref.at[t], back_ref.at[me], send_b, recv_b, t))
+
+    @pl.when(step == 3 * xl + msteps - 1)
+    def _():
         await_all(rs_ref, recv_s)
         await_all(rs_ref, send_s)
         total = rs_ref[0]
@@ -543,6 +552,9 @@
                 spec_ref[lax.rem(h + half, dp), 1, c] = s[h * mh : (h + 1) * mh]
         mine_ref[...] = spec_ref[0]
         theirs_ref[...] = spec_ref[1]
+        pltpu.make_async_copy(sb_ref.at[me], back_ref.at[me], local).wait()
+        await_all(sb_ref, send_b)
+        await_all(sb_ref, recv_b)
 
 
 def pair_weight_kernel(mine_ref, other_ref, eo_ref, ei_ref, out_ref, *, step):
@@ -566,7 +578,7 @@
         out_ref[u, :, C * C :] = imag
 
 
-def restore_kernel(b_ref, sk_ref, yi_ref, zi_ref, out_ref, re_ref, im_ref):
+def restore_kernel(b_ref, sk0_ref, sk1_ref, yi_ref, zi_ref, out_ref, re_ref, im_ref):
     hi, lo = split(b_ref.reshape(MZ * C, 2 * MY)[...])
     v = nn(jnp.concatenate([hi, lo, hi], 1), yi_ref[...])
     re_ref[...] = v[:, :N]
@@ -581,10 +593,11 @@
             turned.append(jnp.concatenate(pieces, 0).T)
         hi, lo = split(jnp.concatenate(turned, 0))
         r = nn(jnp.concatenate([hi, lo, hi], 1), zi_ref[...])
+        sk_ref = sk1_ref if first else sk0_ref
         for k in range(16):
             rows = slice(k // 4 * N, (k // 4 + 1) * N)
             cols = slice(k % 4 * N, (k % 4 + 1) * N)
-            out_ref[0, first + k, 0] = sk_ref[0, first + k, 0] + r[rows, cols]
+            out_ref[0, first + k, 0] = sk_ref[0, k, 0] + r[rows, cols]
 
 
 def fused_body(space, dp, inputs, preact, cotangent, spectral_weight, skip_weight):
@@ -597,6 +610,11 @@
     last = MX // wstep - 1
     nbytes = inputs.size * 4
 
+    late = 2 * xl + MX // wstep
+
+    def twice(s):
+        return (0, 0, jnp.where(s < late, jnp.clip(s - xl, 0, xl - 1), s - late), 0, 0)
+
     def plane(first):
         return pl.BlockSpec((1, C, 1, N, N), lambda s: (0, 0, jnp.clip(s - first, 0, xl - 1), 0, 0))
 
@@ -605,13 +623,13 @@
     half_shape = (2, C, mh, 2 * MY)
     spec_shape = (dp,) + half_shape
     dma = pltpu.SemaphoreType.DMA
-    skip_term, mine, send_half, summed, along = pl.pallas_call(
+    skip_term, mine, send_half, summed, back = pl.pallas_call(
         functools.partial(fused_kernel, space=space, dp=dp, xl=xl, wstep=wstep),
-        grid=(2 * xl + MX // wstep,),
+        grid=(late + xl,),
         in_specs=[
             plane(0),
             plane(0),
-            plane(xl),
+            pl.BlockSpec((1, C, 1, N, N), twice),
             pl.BlockSpec(
                 (wstep, kl, 2 * C * C), lambda s: (jnp.clip(s - 2 * xl, 0, last), 0, 0)
             ),
@@ -623,11 +641,11 @@
             whole(t["eo"].shape),
         ],
         out_specs=[
-            plane(xl),
+            plane(late),
             whole(half_shape),
             whole(half_shape),
             whole((C, 128)),
-            whole(arrive),
+            pl.BlockSpec(memory_space=pl.ANY),
         ],
         out_shape=[
             field,
@@ -642,6 +660,7 @@
             pltpu.VMEM((8 * C, 8 * C), F32),
             pltpu.VMEM(send, F32),
             pltpu.VMEM(send, F32),
+            pltpu.VMEM(arrive, F32),
             pltpu.VMEM(spec_shape, F32),
             pltpu.VMEM(arrive, F32),
             pltpu.VMEM(arrive, F32),
@@ -649,7 +668,7 @@
             pltpu.VMEM((C, 128), F32),
             pltpu.VMEM((space, C, 128), F32),
         ]
-        + [dma] * 6,
+        + [dma] * 9,
         compiler_params=pltpu.CompilerParams(
             vmem_limit_bytes=FUSED_LIMIT, collective_id=0, has_side_effects=True
         ),
@@ -660,7 +679,6 @@
         t["zf"], t["yf"], t["xf"], t["xi"], t["eo"],
     )
     pairs = [(0, 1), (1, 0)]
-    back = lax.all_to_all(along, "space", split_axis=0, concat_axis=0, tiled=True)
     theirs = lax.ppermute(send_half, "dp", pairs)
     skip_grad = NORM * (summed + lax.ppermute(summed, "dp", pairs))[:, :C]
     input_grad = pl.pallas_call(
@@ -668,7 +686,8 @@
         grid=(xl,),
         in_specs=[
             pl.BlockSpec((MZ, 1, C, 2 * MY), lambda x: (0, x, 0, 0)),
-            pl.BlockSpec((1, C, 1, N, N), lambda x: (0, 0, x, 0, 0)),
+            pl.BlockSpec((1, C // 2, 1, N, N), lambda x: (0, 0, x, 0, 0)),
+            pl.BlockSpec((1, C // 2, 1, N, N), lambda x: (0, 1, x, 0, 0)),
             whole(t["yi"].shape),
             whole(t["zi4"].shape),
         ],
@@ -678,7 +697,7 @@
         compiler_params=params(),
         cost_estimate=cost(nbytes * 300, nbytes * 2),
         name="inverse",
-    )(back, skip_term, t["yi"], t["zi4"])
+    )(back, skip_term, skip_term, t["yi"], t["zi4"])
     step = 2
     weight_grad = pl.pallas_call(
         functools.partial(pair_weight_kernel, step=step),

time: 185 us -> 187 us (1.011)
  Pallas kernels: 138 us -> 182 us
  waiting for transfers between devices: 35.4 us -> 0.01 us
  starting transfers between devices: 7.55 us -> 1.53 us
    pallas_call x1, Pallas kernels: 113 us -> 156 us  [fused_body(): pl.pallas_call(functools.partial(fused_kernel, space=space, dp=dp, xl=xl,...]
    all_to_all x1 -> x0, waiting for transfers between devices: 23.2 us -> none  [fused_body(): lax.all_to_all(along, 'space', split_axis=0, concat_axis=0, tiled=True)]
    ppermute x1, waiting for transfers between devices: 12.2 us -> 0.01 us  [fused_body(): skip_grad = NORM * (summed + lax.ppermute(summed, 'dp', pairs))[:, :C]]
    all_to_all x1 -> x0, starting transfers between devices: 6.08 us -> none  [fused_body(): lax.all_to_all(along, 'space', split_axis=0, concat_axis=0, tiled=True)]
  transfers between devices with their start and end apart: 3 -> 2, of which waited for: 2 -> 0; matrix products, arithmetic and copies ran while one was open for 1% -> 0% of each run, Pallas kernels for 4% -> 9%
where the time goes in v4:
time: 187 us; the launch traced here: 186 us
  Pallas kernels  182 us (97%)
    pallas_call x1, Pallas kernels, fused_body(): pl.pallas_call(functools.partial(fused_kernel, space=space, dp=dp, xl=xl,...  156 us
    pallas_call x1, Pallas kernels, fused_body(): pl.pallas_call(restore_kernel, grid=(xl,), in_specs=[pl.BlockSpec((MZ, 1,...  17.2 us
    pallas_call x1, Pallas kernels, fused_body(): pl.pallas_call(functools.partial(pair_weight_kernel, step=step), grid=(mh...  8.19 us
  transfers between devices with their start and end apart: 2, of which 0 were waited for; matrix products, arithmetic and copies ran while one was open for 0% of the time, Pallas kernels for 9%

profile of v4, /device:TPU:15, one launch (start us, length us, event | category | flops | bytes accessed | tf_op | source)
XLA Modules:
  0.0 186.2 jit_solution(8581949703025748859)
XLA Ops:
  0.6 0.0 copy-start.2
  0.6 0.0 copy-start.3
  0.7 156.4 %fused_forward.1 = (f32[1,32,8,128,128]{4,3,2,1,0:T(8,128)}, f32[2,32,16,128]{3,2,1,0:T(8,128)}, f32[2,32,16,128]{3,2,1,0:T(8,128)}, f32[32,128]{1,0:T(8,128)}, f32[16,8,32,128]{3,2,1,0:T(8,128)}) custom-call(f32[1,32,8,128,128]{4,3,2,1,0:T(8,128)} %pre_ref.1, f32[1,32,8,128,128]{4,3,2,1,0:T(8,128)} %cot_ref.1, f32[1,32,8,128,128]{4,3,2,1,0:T(8,128)} %in_ref.1, ...), custom_call_target="tpu_custom_call" | custom-call | flops 25165824000 | bytes 83886080 | tf_op jit(solution)/shard_map/fused_forward/pallas_call | solution.py:626
  157.1 0.3 collective-permute-start.1
  157.4 1.2 collective-permute-start
  158.6 0.0 copy-done.2
  158.6 0.0 copy-done.3
  158.6 0.0 copy-start
  158.6 1.6 copy-done
  160.2 0.0 copy-start.6
  160.2 0.0 copy-start.1
  160.2 0.0 copy-start.4
  160.2 0.0 copy-start.5
  160.2 17.2 %inverse.1 = f32[1,32,8,128,128]{4,3,2,1,0:T(8,128)} custom-call(f32[16,8,32,128]{3,2,1,0:T(8,128)S(1)} %copy-done, f32[1,32,8,128,128]{4,3,2,1,0:T(8,128)} %get-tuple-element.9.sk0_ref.sk1_ref, f32[1,32,8,128,128]{4,3,2,1,0:T(8,128)} %get-tuple-element.9.sk0_ref.sk1_ref, bf16[384,256]{1,0:T(8,128)(2,1)S(1)} %copy-done.3, bf16[384,512]{1,0:T(8,128)(2,1)S(1)} %copy-done.2), custom_call_target="tpu_custom_call" | custom-call | flops 5033164800 | bytes 33554432 | tf_op jit(solution)/shard_map/inverse/pallas_call | solution.py:684
  177.4 0.0 collective-permute-done.1
  177.4 0.0 copy-done.6
  177.4 0.6 fusion
  178.0 0.0 collective-permute-done.other_ref
  178.0 0.0 copy-done.1
  178.0 0.0 copy-done.4
  178.0 0.0 copy-done.5
  178.0 8.2 %weight_grad.1 = f32[16,64,2048]{2,1,0:T(8,128)} custom-call(f32[2,32,16,128]{3,2,1,0:T(8,128)S(1)} %copy-done.1, f32[2,32,16,128]{3,2,1,0:T(8,128)S(1)} %collective-permute-done.other_ref, bf16[64,1024]{1,0:T(8,128)(2,1)S(1)} %copy-done.4, bf16[64,1024]{1,0:T(8,128)(2,1)S(1)} %copy-done.5), custom_call_target="tpu_custom_call" | custom-call | flops 1000000000 | bytes 8388608 | tf_op jit(solution)/shard_map/weight_grad/pallas_call | solution.py:702
Async XLA Ops:
  0.6 158.0 %copy-start.2 = (bf16[384,512]{1,0:T(8,128)(2,1)S(1)}, bf16[384,512]{1,0:T(8,128)(2,1)}, u32[]{:S(2)}) copy-start(bf16[384,512]{1,0:T(8,128)(2,1)} %constant.23.clone.zi_ref) | copy-start | bytes 1179652
  0.6 157.9 %copy-start.3 = (bf16[384,256]{1,0:T(8,128)(2,1)S(1)}, bf16[384,256]{1,0:T(8,128)(2,1)}, u32[]{:S(2)}) copy-start(bf16[384,256]{1,0:T(8,128)(2,1)} %constant.22.clone.yi_ref) | copy-start | bytes 589828
  157.1 20.3 %collective-permute-start.1 = (f32[32,128]{1,0:T(8,128)}, f32[32,128]{1,0:T(8,128)S(1)}, u32[]{:S(2)}, u32[]{:S(2)}) collective-permute-start(f32[32,128]{1,0:T(8,128)} %get-tuple-element.12), channel_id=1, source_target_pairs={{0,16},{16,0},{1,17},{17,1},{2,18},{18,2},{3,19},{19,3},{4,20},{20... | collective-permute-start | bytes 49160 | tf_op jit(solution)/shard_map/ppermute | solution.py:683
  157.4 20.6 %collective-permute-start = (f32[2,32,16,128]{3,2,1,0:T(8,128)}, f32[2,32,16,128]{3,2,1,0:T(8,128)S(1)}, u32[]{:S(2)}, u32[]{:S(2)}) collective-permute-start(f32[2,32,16,128]{3,2,1,0:T(8,128)} %get-tuple-element.11), channel_id=1, source_target_pairs={{0,16},{16,0},{1,17},{17,1},{2,18},{18,2},{3,19},{19,3},{4,20},{20... | collective-permute-start | bytes 1572872 | tf_op jit(solution)/shard_map/ppermute | solution.py:682
  158.6 1.6 copy-start
  160.2 17.2 %copy-start.6 = (f32[32,128]{1,0:T(8,128)S(1)}, f32[32,128]{1,0:T(8,128)}, u32[]{:S(2)}) copy-start(f32[32,128]{1,0:T(8,128)} %get-tuple-element.12) | copy-start | bytes 49156
  160.2 17.8 %copy-start.1 = (f32[2,32,16,128]{3,2,1,0:T(8,128)S(1)}, f32[2,32,16,128]{3,2,1,0:T(8,128)}, u32[]{:S(2)}) copy-start(f32[2,32,16,128]{3,2,1,0:T(8,128)} %get-tuple-element.10.mine_ref) | copy-start | bytes 1572868
  160.2 17.8 %copy-start.4 = (bf16[64,1024]{1,0:T(8,128)(2,1)S(1)}, bf16[64,1024]{1,0:T(8,128)(2,1)}, u32[]{:S(2)}) copy-start(bf16[64,1024]{1,0:T(8,128)(2,1)} %constant.24.clone.eo_ref) | copy-start | bytes 393220
  160.2 17.8 %copy-start.5 = (bf16[64,1024]{1,0:T(8,128)(2,1)S(1)}, bf16[64,1024]{1,0:T(8,128)(2,1)}, u32[]{:S(2)}) copy-start(bf16[64,1024]{1,0:T(8,128)(2,1)} %constant.25.clone.ei_ref) | copy-start | bytes 393220
